TPU v7x, 32 devices: a whole 2x2x4 slice. The times are simulated.
32 devices in a mesh: groups: 2 (over y), pulse: 4 (over x, core), range: 4 (over z).
Axes of the slice: x: 2, y: 2, z: 4, core: 2. Of those that a mesh axis runs over, the one named last changes fastest.
Arguments:
- echoes: bfloat16 [2048, 2, 8192], P(('groups', 'pulse'), None, 'range'), parts along dimension 0, may hold values from -6 to 6
- shifts: int32 [2048], P(('groups', 'pulse')), parts along dimension 0, may hold values from -64 to 64
- tap_weights: float32 [2048, 8], P(('groups', 'pulse')), parts along dimension 0, may hold values from -2 to 2
- angles: float32 [2048], P(('groups', 'pulse')), parts along dimension 0, may hold values from -3.140625 to 3.140625
- slopes: float32 [2048], P(('groups', 'pulse')), parts along dimension 0, may hold values from -0.05 to 0.05
- steering: bfloat16 [2, 8, 32], replicated, may hold values from -0.75 to 0.75
- footprint: int32 [32, 32], P('groups'), parts along dimension 0, may hold values from 0 to 255, as said below
- tile_coeffs: bfloat16 [32, 2, 64, 32], P(('groups', 'pulse')), parts along dimension 0, may hold values from -0.75 to 0.75
Outputs:
- image_tiles: bfloat16 [32, 2, 64, 8192], P(('groups', 'pulse'), None, None, 'range'), parts along dimension 0
There are 2 independent parts, one for each index of `groups`. A program takes and returns all parts, laid end to end along the dimension named above; an argument that names none is the same for every part. Nothing has to cross between parts.
Inputs may be any that keep to these rules, and one draw needn't show every extreme that they name: `footprint`: beam s * 8 + b belongs to subaperture s. The 128 entries of tiles k * 4 to k * 4 + 3 are distinct beams; at most 64 of them lie in any one range of beams j * 64 to j * 64 + 63, and for every k exactly 64 lie in some such range.
All inputs are finite; a program needn't handle non-finite values.
Results may differ from a plain program's by a relative error of at most 0.0058.
Values may be sent and summed in bfloat16 or wider, within the bound.
A program may use at most 64 MiB of HBM per device.

v0:
```python
import jax
import jax.numpy as jnp
from jax import lax
from jax.sharding import PartitionSpec as P

SUB = 32
TAPS = 8
MAXS = 64
TILE_DEV = 4
FOOT = 32
HALO = 68


def padded_2(cells, sides, width):
    for axis, dim in sides:
        count = lax.axis_size(axis)
        ends = count - 1
        head = lax.slice_in_dim(cells, 0, width, axis=dim)
        tail = lax.slice_in_dim(cells, cells.shape[dim] - width, cells.shape[dim], axis=dim)
        cells = jnp.concatenate(
            [
                lax.ppermute(tail, axis, [(i, (i + 1) % count) for i in range(ends)]),
                cells,
                lax.ppermute(head, axis, [((i + 1) % count, i) for i in range(ends)]),
            ],
            axis=dim,
        )
    return cells


def align_block(padded, shifts, tap_weights, angles, slopes, start_cell):
    pulse_rows = padded.shape[0]
    span_cells = padded.shape[2] - 2 * HALO
    reach = 2 * MAXS + TAPS
    offsets = jnp.arange(reach, dtype=jnp.int32)
    tap_where = shifts[:, None] + MAXS + jnp.arange(TAPS, dtype=jnp.int32)[None, :]
    kernel = jnp.sum(
        jnp.where(
            offsets[None, None, :] == tap_where[:, :, None],
            tap_weights[:, :, None],
            jnp.float32(0.0),
        ),
        axis=1,
    )
    kernel = jnp.repeat(kernel, 2, axis=0)[:, None, :]
    source = padded[:, :, 1:].astype(jnp.float32).reshape(1, pulse_rows * 2, span_cells + reach - 1)
    summed = lax.conv_general_dilated(
        source,
        kernel,
        (1,),
        "VALID",
        dimension_numbers=("NCH", "OIH", "NCH"),
        feature_group_count=pulse_rows * 2,
        precision=lax.Precision.HIGHEST,
    )
    summed = summed.reshape(pulse_rows, 2, span_cells)
    positions = (start_cell + jnp.arange(span_cells)).astype(jnp.float32)
    phases = angles[:, None] + slopes[:, None] * positions[None, :]
    cosine_values = jnp.cos(phases)
    sine_values = jnp.sin(phases)
    real_part = cosine_values * summed[:, 0] - sine_values * summed[:, 1]
    imag_part = sine_values * summed[:, 0] + cosine_values * summed[:, 1]
    return jnp.stack([real_part, imag_part], axis=1).astype(jnp.bfloat16)


def project(picked, tile_coeffs):
    weight_real = tile_coeffs[:, 0]
    weight_imag = tile_coeffs[:, 1]
    real_in = picked[:, :, 0]
    imag_in = picked[:, :, 1]
    real_part = jnp.einsum(
        "taf,tfw->taw", weight_real, real_in, preferred_element_type=jnp.float32
    ) - jnp.einsum("taf,tfw->taw", weight_imag, imag_in, preferred_element_type=jnp.float32)
    imag_part = jnp.einsum(
        "taf,tfw->taw", weight_real, imag_in, preferred_element_type=jnp.float32
    ) + jnp.einsum("taf,tfw->taw", weight_imag, real_in, preferred_element_type=jnp.float32)
    return jnp.stack([real_part, imag_part], axis=1).astype(jnp.bfloat16)


def body(echoes, shifts, tap_weights, angles, slopes, steering, footprint, tile_coeffs):
    cells = echoes.shape[2]
    padded = padded_2(echoes, (("range", 2),), HALO)
    start_cell = lax.axis_index("range") * cells
    aligned = align_block(padded, shifts, tap_weights, angles, slopes, start_cell)
    groups = aligned.reshape(aligned.shape[0] // SUB, SUB, 2, cells)
    real_in = groups[:, :, 0]
    imag_in = groups[:, :, 1]
    real_part = jnp.einsum(
        "bj,sjw->sbw", steering[0], real_in, preferred_element_type=jnp.float32
    ) - jnp.einsum("bj,sjw->sbw", steering[1], imag_in, preferred_element_type=jnp.float32)
    imag_part = jnp.einsum(
        "bj,sjw->sbw", steering[0], imag_in, preferred_element_type=jnp.float32
    ) + jnp.einsum("bj,sjw->sbw", steering[1], real_in, preferred_element_type=jnp.float32)
    beam_rows = jnp.stack([real_part, imag_part], axis=2).astype(jnp.bfloat16)
    beam_rows = beam_rows.reshape(-1, 2, cells)
    pulse_count = lax.axis_size("pulse")
    my_index = lax.axis_index("pulse")
    entries = TILE_DEV * FOOT
    owner_ids = footprint.reshape(pulse_count, entries)
    my_entries = lax.dynamic_index_in_dim(owner_ids, my_index, 0, keepdims=False)
    gathered = lax.all_gather(beam_rows, "pulse", axis=0, tiled=True)
    picked = jnp.take(gathered, my_entries, axis=0).reshape(TILE_DEV, FOOT, 2, cells)
    image_tiles = project(picked, tile_coeffs)
    return image_tiles


def solution(mesh):
    placed = (
        P(("groups", "pulse"), None, "range"),
        P(("groups", "pulse")),
        P(("groups", "pulse"), None),
        P(("groups", "pulse")),
        P(("groups", "pulse")),
        P(),
        P("groups", None),
        P(("groups", "pulse"), None, None, None),
    )
    return jax.shard_map(
        body,
        mesh=mesh,
        in_specs=placed,
        out_specs=P(("groups", "pulse"), None, None, "range"),
        check_vma=False,
    )
```

profile of v0, /device:TPU:1, one launch (start us, length us, event | category | flops | bytes accessed | tf_op | source)
XLA Modules:
  0.0 247.3 jit_solution(8722996066743790988)
XLA Ops:
  6.5 0.0 all-gather.2.cloned.1.call-start
  6.5 1.2 fusion.47
  7.8 4.0 %collective-permute-start = (bf16[256,2,68]{2,1,0:T(2,128)(2,1)S(1)}, bf16[256,2,68]{2,1,0:T(2,128)(2,1)S(1)}, u32[]{:S(2)}, u32[]{:S(2)}) collective-permute-start(bf16[256,2,68]{2,1,0:T(2,128)(2,1)S(1)} %get-tuple-element.10), channel_id=1, source_target_pairs={{0,1},{1,2},{2,3},{4,5},{5,6},{6,7},{8,9},{9,10},{10,11},{12,13},{... | collective-permute-start | bytes 208904 | tf_op jit(solution)/shard_map/ppermute | solution.py:22
  11.8 1.3 collective-permute-start.1
  13.1 0.7 broadcast_add_fusion
  13.8 0.8 select_reduce_fusion
  14.6 0.1 copy.68
  14.8 0.2 broadcast_in_dim.36
  15.0 0.4 broadcast_in_dim_reshape.3
  15.3 0.2 copy.69
  15.5 0.0 collective-permute-done
  15.5 2.0 collective-permute-done.1
  17.5 14.3 %concatenate.7 = bf16[256,2,2184]{2,1,0:T(2,128)(2,1)S(1)} concatenate(bf16[256,2,68]{2,1,0:T(2,128)(2,1)S(1)} %collective-permute-done, bf16[256,2,2048]{2,1,0:T(2,128)(2,1)} %param.8, bf16[256,2,68]{2,1,0:T(2,128)(2,1)S(1)} %collective-permute-done.1), dimensions={2} | concatenate | bytes 4472832 | tf_op jit(solution)/shard_map/concatenate | solution.py:20
  31.9 6.5 %slice.54 = bf16[256,2,2183]{2,1,0:T(2,128)(2,1)} slice(bf16[256,2,2184]{2,1,0:T(2,128)(2,1)S(1)} %concatenate.7), slice={[0:256], [0:2], [1:2184]} | slice | bytes 4470784 | tf_op jit(solution)/shard_map/slice | solution.py:46
  38.4 4.9 %reshape.215 = bf16[512,1,2183]{2,0,1:T(8,128)(2,1)S(1)} reshape(bf16[256,2,2183]{2,1,0:T(2,128)(2,1)} %slice.54) | data formatting | bytes 4470784 | tf_op jit(solution)/shard_map/reshape | solution.py:46
  43.3 1.7 pad
  45.0 6.8 %reshape.230 = bf16[512,1,8,273]{3,2,0,1:T(8,128)(2,1)} reshape(bf16[512,1,2184]{2,0,1:T(8,128)(2,1)} %pad) | data formatting | bytes 4472832 | tf_op jit(solution)/shard_map/conv_general_dilated | solution.py:47
  51.8 4.4 %copy.67 = bf16[512,1,8,273]{0,2,3,1:T(8,128)(2,1)S(1)} copy(bf16[512,1,8,273]{3,2,0,1:T(8,128)(2,1)} %reshape.230) | data formatting | bytes 4472832 | tf_op jit(solution)/shard_map/conv_general_dilated | solution.py:47
  56.2 0.3 slice.55
  56.4 0.0 copy-start.5
  56.4 0.3 fusion.56
  56.8 0.4 copy-done.5
  57.2 103.2 %broadcast_select_fusion = f32[8,273,512]{2,0,1:T(8,128)S(1)} fusion(pred[8,273]{0,1:T(8,128)(4,1)S(1)} %copy-done.5, f32[512,1,136]{0,1,2:T(1,128)S(1)} %copy.69, bf16[512,8,408]{0,1,2:T(8,128)(2,1)S(1)} %fusion.56), kind=kOutput, calls=%fused_computation.22 | convolution fusion | flops 1826033664 | bytes 8095880 | tf_op jit(solution)/shard_map/conv_general_dilated | solution.py:47
  160.4 4.7 %copy.70 = f32[8,273,512]{2,1,0:T(8,128)} copy(f32[8,273,512]{2,0,1:T(8,128)S(1)} %broadcast_select_fusion) | data formatting | bytes 8945664 | tf_op jit(solution)/shard_map/conv_general_dilated | solution.py:47
  165.1 5.1 %reshape.214 = f32[1,2184,512]{2,1,0:T(8,128)} reshape(f32[8,273,512]{2,1,0:T(8,128)} %copy.70) | data formatting | bytes 8945664 | tf_op jit(solution)/shard_map/conv_general_dilated | solution.py:47
  170.2 4.6 %slice_bitcast_fusion = f32[1,512,2048]{1,2,0:T(8,128)} fusion(f32[1,2184,512]{2,1,0:T(8,128)} %reshape.214), kind=kLoop, calls=%fused_computation.3 | loop fusion | bytes 8388608 | tf_op jit(solution)/shard_map/conv_general_dilated | solution.py:47
  174.8 5.5 %copy.71 = f32[1,512,2048]{2,1,0:T(8,128)} copy(f32[1,512,2048]{1,2,0:T(8,128)} %slice_bitcast_fusion) | data formatting | bytes 8388608 | tf_op jit(solution)/shard_map/conv_general_dilated | solution.py:47
  180.2 5.8 %reshape.207 = f32[256,2,2048]{2,1,0:T(2,128)} reshape(f32[1,512,2048]{2,1,0:T(8,128)} %copy.71) | data formatting | bytes 8388608 | tf_op jit(solution)/shard_map/reshape | solution.py:56
  186.0 0.0 copy-start.3
  186.0 0.0 copy-start.4
  186.0 7.8 %fusion.46 = (f32[256,1,2048]{2,1,0:T(1,128)S(1)}, f32[256,1,2048]{2,1,0:T(1,128)S(1)}) fusion(f32[256,2,2048]{2,1,0:T(2,128)} %reshape.207), kind=kLoop, calls=%fused_computation.69 | loop fusion | bytes 8388608 | tf_op jit(solution)/shard_map/slice | solution.py:61
  193.8 0.0 copy-done.3
  193.8 0.0 copy-done.4
  193.9 0.0 copy-start.1
  193.9 9.1 %subtract_convert_fusion = (bf16[256,1,2048]{2,0,1:T(8,128)(2,1)S(1)}, bf16[256,1,2048]{2,0,1:T(8,128)(2,1)S(1)}) fusion(f32[256,1,2048]{2,1,0:T(1,128)S(1)} %get-tuple-element.8, f32[256,1,2048]{2,1,0:T(1,128)S(1)} %get-tuple-element.7, f32[2048]{0:T(1024)S(1)} %add_convert_fusion.1, f32[256]{0:T(256)S(1)} %copy-done.3, f32[256]{0:T(256)S(1)} %copy-done.4), kind=kLoop, calls=%fused_computation.25 | loop fusion | flops 5242880 | bytes 6301696 | tf_op jit(solution)/shard_map/convert.15
  203.0 0.0 copy-done.1
  203.0 0.3 fusion.35
  203.3 0.3 fusion.33
  203.6 0.3 fusion.15
  203.8 0.4 copy.74
  204.2 0.0 copy-start.2
  204.2 0.3 fusion.14
  204.5 0.4 copy.75
  204.9 2.0 pad_maximum_fusion.1
  206.9 0.0 all-gather.2.cloned.1.call-update
  206.9 0.0 copy-done.2
  206.9 0.1 reshape.205
  207.1 0.1 squeeze.36
  207.2 24.6 %all-gather.2.cloned.1.call-done = bf16[256,2,2048]{2,1,0:T(2,128)(2,1)} async-done(((bf16[64,2,2048]{2,1,0:T(2,128)(2,1)}), bf16[256,2,2048]{2,1,0:T(2,128)(2,1)}) %all-gather.2.cloned.1.call-update) | async-done | bytes 2097168 | tf_op jit(solution)/shard_map/all_gather | solution.py:101
  231.7 4.3 %gather_fusion = bf16[128,2,2048]{2,1,0:T(2,128)(2,1)S(1)} fusion(bf16[256,2,2048]{2,1,0:T(2,128)(2,1)} %all-gather.2.cloned.1.call-done, s32[1024]{0:T(1024)S(1)} %pad_clamp_fusion), kind=kCustom, calls=%fused_computation | custom fusion | bytes 2097664 | tf_op jit(solution)/shard_map/jit(_take)/gather | solution.py:102
  236.0 0.0 copy-start
  236.0 0.4 copy.76
  236.4 0.2 broadcast_select_fusion.1
  236.5 0.3 copy-done
  236.9 0.5 fusion.21
  237.3 0.5 fusion.22
  237.8 0.5 fusion.11
  238.3 0.5 fusion.10
  238.8 0.2 pad_maximum_fusion
  239.0 1.5 copy.79
  (6 shorter events, 0.1 us)
Async XLA Ops:
  6.5 225.2 %all-gather.2.cloned.1.call-start = ((), (), s32[]{:S(2)}) async-start(), calls=%async_computation | async-start | bytes 2621440 | tf_op jit(solution)/shard_map/all_gather | solution.py:101
  7.8 7.8 %collective-permute-start = (bf16[256,2,68]{2,1,0:T(2,128)(2,1)S(1)}, bf16[256,2,68]{2,1,0:T(2,128)(2,1)S(1)}, u32[]{:S(2)}, u32[]{:S(2)}) collective-permute-start(bf16[256,2,68]{2,1,0:T(2,128)(2,1)S(1)} %get-tuple-element.10), channel_id=1, source_target_pairs={{0,1},{1,2},{2,3},{4,5},{5,6},{6,7},{8,9},{9,10},{10,11},{12,13},{... | collective-permute-start | bytes 208904 | tf_op jit(solution)/shard_map/ppermute | solution.py:22
  11.8 5.7 %collective-permute-start.1 = (bf16[256,2,68]{2,1,0:T(2,128)(2,1)S(1)}, bf16[256,2,68]{2,1,0:T(2,128)(2,1)S(1)}, u32[]{:S(2)}, u32[]{:S(2)}) collective-permute-start(bf16[256,2,68]{2,1,0:T(2,128)(2,1)S(1)} %get-tuple-element.9), channel_id=1, source_target_pairs={{1,0},{2,1},{3,2},{5,4},{6,5},{7,6},{9,8},{10,9},{11,10},{13,12},{... | collective-permute-start | bytes 208904 | tf_op jit(solution)/shard_map/ppermute | solution.py:24
  56.4 0.8 copy-start.5
  186.0 7.8 %copy-start.3 = (f32[256]{0:T(256)S(1)}, f32[256]{0:T(256)}, u32[]{:S(2)}) copy-start(f32[256]{0:T(256)} %param.12) | copy-start | bytes 3076
  186.0 7.8 %copy-start.4 = (f32[256]{0:T(256)S(1)}, f32[256]{0:T(256)}, u32[]{:S(2)}) copy-start(f32[256]{0:T(256)} %param.11) | copy-start | bytes 3076
  193.9 9.2 %copy-start.1 = (bf16[2,8,32]{2,1,0:T(8,128)(2,1)S(1)}, bf16[2,8,32]{2,1,0:T(8,128)(2,1)}, u32[]{:S(2)}) copy-start(bf16[2,8,32]{2,1,0:T(8,128)(2,1)} %param.13) | copy-start | bytes 3076
  204.2 2.7 %copy-start.2 = (s32[16,32]{1,0:T(8,128)S(1)}, s32[16,32]{1,0:T(8,128)}, u32[]{:S(2)}) copy-start(s32[16,32]{1,0:T(8,128)} %param.14) | copy-start | bytes 6148
  236.0 0.8 copy-start
Sparse Core Ops, SparseCore 0:
  207.1 24.6 all-gather.1
where the time goes:
time: 249 us; the launch traced here: 247 us
  matrix products  106 us (43%)
  local copies, waits for them, and re-layouts  82.2 us (33%)
  waiting for transfers between devices  26.6 us (11%)
  between operations  13.7 us (6%)
  other arithmetic  13.4 us (5%)
  starting transfers between devices  5.33 us (2%)
    conv_general_dilated x1, matrix products, align_block(): lax.conv_general_dilated(source, kernel, (1,), 'VALID', dimension_numbers...  103 us
    conv_general_dilated x7, local copies, waits for them, and re-layouts, align_block(): lax.conv_general_dilated(source, kernel, (1,), 'VALID', dimension_numbers...  31.2 us
    all_gather x1, waiting for transfers between devices, body(): gathered = lax.all_gather(beam_rows, 'pulse', axis=0, tiled=True)  24.6 us
    concatenate x1, local copies, waits for them, and re-layouts, padded_2(): jnp.concatenate([lax.ppermute(tail, axis, [(i, (i + 1) % count) for i in...  14.3 us
    another operation x1, other arithmetic  9.14 us
    slice x1, local copies, waits for them, and re-layouts, align_block(): real_part = cosine_values * summed[:, 0] - sine_values * summed[:, 1]  7.79 us
    reshape x2, local copies, waits for them, and re-layouts, align_block(): padded[:, :, 1:].astype(jnp.float32)  6.6 us
    slice x1, local copies, waits for them, and re-layouts, align_block(): padded[:, :, 1:].astype(jnp.float32)  6.51 us
  transfers between devices with their start and end apart: 3, of which 2 were waited for; matrix products, arithmetic and copies ran while one was open for 1% of the time, Pallas kernels for 0%

commit v1 on v0

v1 whole, which is shorter than its diff:
```python
import functools

import jax
import jax.numpy as jnp
from jax import lax
from jax.experimental import pallas as pl
from jax.experimental.pallas import tpu as pltpu
from jax.sharding import PartitionSpec as P

SUB = 32
BEAMS = 8
TAPS = 8
TILE_DEV = 4
FOOT = 32
AZ = 64
LANES = 128
F32 = jnp.float32
BF16 = jnp.bfloat16
MESH_ID = pl.DeviceIdType.MESH
UNROLL = 8


def beam_kernel(
    n_pulse, n_range, blocks, subs,
    shifts, echoes, heads, tails, params, steering, footprint, tile_coeffs,
    gathered, dense,
    cells, left, right, left_f, right_f, rolled, y_re, y_im, taps_out, sent,
    lhs_re, lhs_im, e_re, e_im, d_re, d_im, reach,
    load_sem, halo_send, halo_recv, own_sem,
    x_send, x_recv, sib_send, sib_recv, fwd_send, fwd_recv,
):
    chips = n_pulse // 2
    me = lax.axis_index("pulse")
    zi = lax.axis_index("range")
    gi = lax.axis_index("groups")
    chip = me // 2
    core = me % 2
    sibling = chip * 2 + (1 - core)
    pulses = subs * SUB
    has_left = zi > 0
    has_right = zi < n_range - 1

    def dev(p, z):
        return (gi, p, z)

    load = pltpu.make_async_copy(echoes, cells, load_sem)
    load.start()

    barrier = pltpu.get_barrier_semaphore()
    pl.semaphore_signal(barrier, inc=1, device_id=dev(sibling, zi), device_id_type=MESH_ID)
    for d in range(1, chips):
        peer = ((chip + d) % chips) * 2 + core
        pl.semaphore_signal(barrier, inc=1, device_id=dev(peer, zi), device_id_type=MESH_ID)

    @pl.when(has_left)
    def _():
        pl.semaphore_signal(barrier, inc=1, device_id=dev(me, zi - 1), device_id_type=MESH_ID)

    @pl.when(has_right)
    def _():
        pl.semaphore_signal(barrier, inc=1, device_id=dev(me, zi + 1), device_id_type=MESH_ID)

    pl.semaphore_wait(barrier, chips + jnp.minimum(zi, 1) + jnp.minimum(n_range - 1 - zi, 1))

    def to_left():
        return pltpu.make_async_remote_copy(
            src_ref=heads, dst_ref=right, send_sem=halo_send.at[0], recv_sem=halo_recv.at[0],
            device_id=dev(me, zi - 1), device_id_type=MESH_ID)

    def to_right():
        return pltpu.make_async_remote_copy(
            src_ref=tails, dst_ref=left, send_sem=halo_send.at[1], recv_sem=halo_recv.at[1],
            device_id=dev(me, zi + 1), device_id_type=MESH_ID)

    @pl.when(has_left)
    def _():
        to_left().start()

    @pl.when(has_right)
    def _():
        to_right().start()

    lane = lax.broadcasted_iota(jnp.int32, (LANES, LANES), 1).astype(F32)
    start = (zi * (blocks * LANES)).astype(F32)
    for h in range(pulses // LANES):
        span = pl.ds(h * LANES, LANES)

        def column(row):
            return jnp.transpose(jnp.broadcast_to(params[row:row + 1, span], (LANES, LANES)))

        angle, slope, shift = column(TAPS), column(TAPS + 1), column(TAPS + 2)
        phase = angle + slope * (start + lane)
        e_re[span, :] = jnp.cos(phase)
        e_im[span, :] = jnp.sin(phase)
        step = slope * float(LANES)
        d_re[span, :] = jnp.cos(step)
        d_im[span, :] = jnp.sin(step)
        reach[span, :] = shift + lane + float(LANES - TAPS // 2 + 1)

    tap_phase = params[TAPS + 1:TAPS + 2, :] * lax.broadcasted_iota(jnp.int32, (TAPS, pulses), 0).astype(F32)
    tap_re = params[0:TAPS, :] * jnp.cos(tap_phase)
    tap_im = -params[0:TAPS, :] * jnp.sin(tap_phase)
    st_re = steering[0].astype(F32)
    st_im = steering[1].astype(F32)
    for s in range(subs):
        g_re = tap_re[:, s * SUB:(s + 1) * SUB]
        g_im = tap_im[:, s * SUB:(s + 1) * SUB]
        for k in range(TAPS):
            w_re = st_re * g_re[k:k + 1] - st_im * g_im[k:k + 1]
            w_im = st_re * g_im[k:k + 1] + st_im * g_re[k:k + 1]
            rows = pl.ds(k * 2 * BEAMS, 2 * BEAMS)
            lhs_re[s, rows, :] = jnp.concatenate([w_re, w_im], axis=0).astype(BF16)
            lhs_im[s, rows, :] = jnp.concatenate([-w_im, w_re], axis=0).astype(BF16)

    @pl.when(has_left)
    def _():
        to_right().wait_recv()

    @pl.when(has_right)
    def _():
        to_left().wait_recv()

    @pl.when(jnp.logical_not(has_left))
    def _():
        left[...] = jnp.zeros(left.shape, BF16)

    @pl.when(jnp.logical_not(has_right))
    def _():
        right[...] = jnp.zeros(right.shape, BF16)

    left_f[...] = left[...].astype(F32)
    right_f[...] = right[...].astype(F32)
    load.wait()

    def x_copy(d, s):
        peer = ((chip + d) % chips) * 2 + core
        return pltpu.make_async_remote_copy(
            src_ref=sent.at[s], dst_ref=gathered.at[me, s],
            send_sem=x_send.at[d - 1, s], recv_sem=x_recv.at[d - 1, s],
            device_id=dev(peer, zi), device_id_type=MESH_ID)

    def sib_copy(s):
        return pltpu.make_async_remote_copy(
            src_ref=sent.at[s], dst_ref=gathered.at[me, s],
            send_sem=sib_send.at[s], recv_sem=sib_recv.at[s],
            device_id=dev(sibling, zi), device_id_type=MESH_ID)

    def fwd_copy(d, s):
        owner = ((chip + chips - d) % chips) * 2 + core
        return pltpu.make_async_remote_copy(
            src_ref=gathered.at[owner, s], dst_ref=gathered.at[owner, s],
            send_sem=fwd_send.at[d - 1, s], recv_sem=fwd_recv.at[d - 1, s],
            device_id=dev(sibling, zi), device_id_type=MESH_ID)

    def own_copy(s):
        return pltpu.make_async_copy(sent.at[s], gathered.at[me, s], own_sem.at[s])

    def forward(s):
        for d in range(1, chips):
            x_copy(d, s).wait_recv()
            fwd_copy(d, s).start()

    own_rows = 2 * blocks

    def one_sub(s, carry):
        def some_pulses(group, inner):
            for u in range(UNROLL):
                j = group * UNROLL + u
                pulse = s * SUB + j
                amount = (LANES - (shifts[pulse] + (LANES - TAPS // 2 + 1))) & (LANES - 1)
                rolled[0:own_rows, j, :] = pltpu.roll(cells[pulse].astype(F32), amount, axis=1)
                rolled[own_rows:own_rows + 2, j, :] = pltpu.roll(left_f[pl.ds(2 * pulse, 2), :], amount, axis=1)
                rolled[own_rows + 2:own_rows + 4, j, :] = pltpu.roll(right_f[pl.ds(2 * pulse, 2), :], amount, axis=1)
            return inner

        lax.fori_loop(0, SUB // UNROLL, some_pulses, 0)

        rows = pl.ds(pl.multiple_of(s * SUB, SUB), SUB)
        at = reach[rows, :]
        first = at < float(LANES)
        second = at < float(2 * LANES)
        turn_re, turn_im = d_re[rows, :], d_im[rows, :]
        now_re, now_im = e_re[rows, :], e_im[rows, :]

        def block(b, c):
            b = min(b, blocks + 1)
            where = own_rows if b == 0 else own_rows + 2 if b == blocks + 1 else 2 * (b - 1)
            return rolled[where + c]

        for b in range(blocks + 1):
            z = [
                jnp.where(first, block(b, c), jnp.where(second, block(b + 1, c), block(b + 2, c)))
                for c in range(2)
            ]
            span = slice(b * LANES, (b + 1) * LANES)
            y_re[:, span] = (now_re * z[0] - now_im * z[1]).astype(BF16)
            y_im[:, span] = (now_im * z[0] + now_re * z[1]).astype(BF16)
            now_re, now_im = now_re * turn_re - now_im * turn_im, now_im * turn_re + now_re * turn_im

        taps_out[...] = jnp.dot(lhs_re[s], y_re[...], preferred_element_type=F32) + jnp.dot(
            lhs_im[s], y_im[...], preferred_element_type=F32)
        width = (blocks + 1) * LANES
        total = taps_out[0:2 * BEAMS, :]
        for k in range(1, TAPS):
            total = total + pltpu.roll(taps_out[k * 2 * BEAMS:(k + 1) * 2 * BEAMS, :], width - k, axis=1)
        sent[s] = total[:, :blocks * LANES].astype(BF16)

        for d in range(1, chips):
            x_copy(d, s).start()
        sib_copy(s).start()
        own_copy(s).start()

        @pl.when(s >= 2)
        def _():
            forward(s - 2)

        return carry

    lax.fori_loop(0, subs, one_sub, 0)
    forward(subs - 2)

    n_rows = n_pulse * subs * 2 * BEAMS
    row = lax.broadcasted_iota(jnp.int32, (n_rows, FOOT), 0)
    beam = (row // (2 * BEAMS)) * BEAMS + row % BEAMS
    is_im = (row // BEAMS) % 2
    for t in range(TILE_DEV):
        ids = footprint[pl.ds(me * TILE_DEV + t, 1), :]
        hit = beam == ids
        hot_re = jnp.where(hit & (is_im == 0), 1.0, 0.0).astype(BF16)
        hot_im = jnp.where(hit & (is_im == 1), 1.0, 0.0).astype(BF16)
        c_re, c_im = tile_coeffs[t, 0], tile_coeffs[t, 1]

        def spread(a, b):
            return lax.dot_general(a, b, (((1,), (1,)), ((), ())), preferred_element_type=F32)

        dense[t * 2 * AZ:t * 2 * AZ + AZ, :] = (spread(c_re, hot_re) - spread(c_im, hot_im)).astype(BF16)
        dense[t * 2 * AZ + AZ:(t + 1) * 2 * AZ, :] = (spread(c_im, hot_re) + spread(c_re, hot_im)).astype(BF16)

    forward(subs - 1)

    def finish(s, carry):
        own_copy(s).wait()
        sib_copy(s).wait()
        for d in range(1, chips):
            x_copy(d, s).wait_send()
            fwd_copy(d, s).wait()
        return carry

    lax.fori_loop(0, subs, finish, 0)

    @pl.when(has_left)
    def _():
        to_left().wait_send()

    @pl.when(has_right)
    def _():
        to_right().wait_send()


def project_kernel(dense, beams, out):
    out[...] = jnp.dot(dense[...], beams[...], preferred_element_type=F32).astype(BF16)


def body(n_pulse, n_range, echoes, shifts, tap_weights, angles, slopes, steering, footprint, tile_coeffs):
    pulses, _, width = echoes.shape
    blocks = width // LANES
    subs = pulses // SUB
    chips = n_pulse // 2
    by_block = echoes.reshape(pulses, 2, blocks, LANES).transpose(0, 2, 1, 3).reshape(pulses, 2 * blocks, LANES)
    heads = echoes[:, :, :LANES].reshape(2 * pulses, LANES)
    tails = echoes[:, :, width - LANES:].reshape(2 * pulses, LANES)
    params = jnp.concatenate(
        [
            tap_weights.T, angles[None], slopes[None], shifts[None].astype(F32),
            jnp.zeros((5, pulses), F32),
        ],
        axis=0,
    )
    n_rows = n_pulse * subs * 2 * BEAMS
    out_rows = TILE_DEV * 2 * AZ
    vmem = pl.BlockSpec(memory_space=pltpu.VMEM)
    hbm = pl.BlockSpec(memory_space=pl.ANY)
    dma = pltpu.SemaphoreType.DMA
    gathered, dense = pl.pallas_call(
        functools.partial(beam_kernel, n_pulse, n_range, blocks, subs),
        out_shape=(
            jax.ShapeDtypeStruct((n_pulse, subs, 2 * BEAMS, width), BF16),
            jax.ShapeDtypeStruct((out_rows, n_rows), BF16),
        ),
        in_specs=[pl.BlockSpec(memory_space=pltpu.SMEM), hbm, vmem, vmem, vmem, vmem, vmem, vmem],
        out_specs=(hbm, vmem),
        scratch_shapes=[
            pltpu.VMEM((pulses, 2 * blocks, LANES), BF16),
            pltpu.VMEM((2 * pulses, LANES), BF16),
            pltpu.VMEM((2 * pulses, LANES), BF16),
            pltpu.VMEM((2 * pulses, LANES), F32),
            pltpu.VMEM((2 * pulses, LANES), F32),
            pltpu.VMEM((2 * blocks + 4, SUB, LANES), F32),
            pltpu.VMEM((SUB, width + LANES), BF16),
            pltpu.VMEM((SUB, width + LANES), BF16),
            pltpu.VMEM((TAPS * 2 * BEAMS, width + LANES), F32),
            pltpu.VMEM((subs, 2 * BEAMS, width), BF16),
            pltpu.VMEM((subs, TAPS * 2 * BEAMS, SUB), BF16),
            pltpu.VMEM((subs, TAPS * 2 * BEAMS, SUB), BF16),
            pltpu.VMEM((pulses, LANES), F32),
            pltpu.VMEM((pulses, LANES), F32),
            pltpu.VMEM((pulses, LANES), F32),
            pltpu.VMEM((pulses, LANES), F32),
            pltpu.VMEM((pulses, LANES), F32),
            dma(()),
            dma((2,)),
            dma((2,)),
            dma((subs,)),
            dma((chips - 1, subs)),
            dma((chips - 1, subs)),
            dma((subs,)),
            dma((subs,)),
            dma((chips - 1, subs)),
            dma((chips - 1, subs)),
        ],
        compiler_params=pltpu.CompilerParams(
            collective_id=0, has_side_effects=True, vmem_limit_bytes=48 * 1024 * 1024
        ),
    )(shifts, by_block, heads, tails, params, steering, footprint, tile_coeffs)

    columns = 512
    image = pl.pallas_call(
        project_kernel,
        grid=(width // columns,),
        out_shape=jax.ShapeDtypeStruct((out_rows, width), BF16),
        in_specs=[
            pl.BlockSpec((out_rows, n_rows), lambda i: (0, 0)),
            pl.BlockSpec((n_rows, columns), lambda i: (0, i)),
        ],
        out_specs=pl.BlockSpec((out_rows, columns), lambda i: (0, i)),
        compiler_params=pltpu.CompilerParams(vmem_limit_bytes=48 * 1024 * 1024),
    )(dense, gathered.reshape(n_rows, width))
    return image.reshape(TILE_DEV, 2, AZ, width)


def solution(mesh):
    placed = (
        P(("groups", "pulse"), None, "range"),
        P(("groups", "pulse")),
        P(("groups", "pulse"), None),
        P(("groups", "pulse")),
        P(("groups", "pulse")),
        P(),
        P("groups", None),
        P(("groups", "pulse"), None, None, None),
    )
    return jax.shard_map(
        functools.partial(body, mesh.shape["pulse"], mesh.shape["range"]),
        mesh=mesh,
        in_specs=placed,
        out_specs=P(("groups", "pulse"), None, None, "range"),
        check_vma=False,
    )
```

time: 249 us -> 38.2 us (0.15)
  matrix products: 106 us -> 0 us
  local copies, waits for them, and re-layouts: 82.2 us -> 7.18 us
  Pallas kernels: 0 us -> 29.9 us
  waiting for transfers between devices: 26.6 us -> 0 us
  between operations: 13.7 us -> 0.03 us
  other arithmetic: 13.4 us -> 0.68 us
  starting transfers between devices: 5.33 us -> 0 us
    conv_general_dilated x1 -> x0, matrix products: 103 us -> none  [align_block(): lax.conv_general_dilated(source, kernel, (1,), 'VALID', dimension_numbers...]
    conv_general_dilated x7 -> x0, local copies, waits for them, and re-layouts: 31.2 us -> none  [align_block(): lax.conv_general_dilated(source, kernel, (1,), 'VALID', dimension_numbers...]
    pallas_call x0 -> x2, Pallas kernels: none -> 29.9 us  [the longest x1 26.8 us: body(): pl.pallas_call(functools.partial(beam_kernel, n_pulse, n_range, blocks, s...]
    all_gather x1 -> x0, waiting for transfers between devices: 24.6 us -> none  [body(): gathered = lax.all_gather(beam_rows, 'pulse', axis=0, tiled=True)]
    slice x3 -> x1, local copies, waits for them, and re-layouts: 15.5 us -> 1.17 us  [body(): tails = echoes[:, :, width - LANES:].reshape(2 * pulses, LANES)]
    concatenate x1, local copies, waits for them, and re-layouts: 14.3 us -> 1.41 us  [body(): jnp.concatenate([tap_weights.T, angles[None], slopes[None], shifts[None]....]
    reshape x4 -> x0, local copies, waits for them, and re-layouts: 12.5 us -> none  [the longest x2 6.6 us: align_block(): padded[:, :, 1:].astype(jnp.float32)]
    another operation x3 -> x0, other arithmetic: 11.3 us -> none
  transfers between devices with their start and end apart: 3 -> 0, of which waited for: 2 -> 0; matrix products, arithmetic and copies ran while one was open for 1% -> 0% of each run, Pallas kernels for 0% -> 0%
where the time goes in v1:
time: 38.2 us; the launch traced here: 37.8 us
  Pallas kernels  29.9 us (78%)
  local copies, waits for them, and re-layouts  7.18 us (19%)
  other arithmetic  0.68 us (2%)
    pallas_call x1, Pallas kernels, body(): pl.pallas_call(functools.partial(beam_kernel, n_pulse, n_range, blocks, s...  26.8 us
    unnamed x9, local copies, waits for them, and re-layouts  4.6 us
    pallas_call x1, Pallas kernels, body(): pl.pallas_call(project_kernel, grid=(width // columns,), out_shape=jax.Sh...  3.06 us
    concatenate x1, local copies, waits for them, and re-layouts, body(): jnp.concatenate([tap_weights.T, angles[None], slopes[None], shifts[None]....  1.41 us
    slice x1, local copies, waits for them, and re-layouts, body(): tails = echoes[:, :, width - LANES:].reshape(2 * pulses, LANES)  1.17 us

profile of v1, /device:TPU:1, one launch (start us, length us, event | category | flops | bytes accessed | tf_op | source)
XLA Modules:
  0.0 37.8 jit_solution(17722343563120051547)
XLA Ops:
  0.0 0.7 %convert_element_type.6 = f32[256]{0:T(256)S(1)} convert(s32[256]{0:T(256)} %shifts.1) | non-fusion elementwise | flops 256 | bytes 2048 | tf_op jit(solution)/shard_map/convert_element_type | solution.py:274
  0.7 1.4 %concatenate.3.params = f32[16,256]{1,0:T(8,128)S(1)} concatenate(f32[8,256]{1,0:T(8,128)} %bitcast.17, f32[1,256]{1,0:T(1,128)} %bitcast.19, f32[1,256]{1,0:T(1,128)} %bitcast.20, f32[1,256]{1,0:T(1,128)S(1)} %bitcast.18, f32[5,256]{1,0:T(8,128)S(1)} %broadcast_in_dim.12), dimensions={0} | concatenate | bytes 32768 | tf_op jit(solution)/shard_map/concatenate | solution.py:272
  2.1 1.0 %copy.10.tile_coeffs = bf16[4,2,64,32]{3,2,1,0:T(8,128)(2,1)S(1)} copy(bf16[4,2,64,32]{2,3,1,0:T(8,128)(2,1)} %param.15) | data formatting | bytes 65536 | tf_op args[7]
  3.1 1.2 %fusion = (bf16[256,2,128]{2,1,0:T(2,128)(2,1)S(1)}, bf16[256,2,128]{2,1,0:T(2,128)(2,1)S(1)}) fusion(bf16[256,2,2048]{2,1,0:T(2,128)(2,1)} %param.8), kind=kLoop, calls=%fused_computation | loop fusion | bytes 524288 | tf_op jit(solution)/shard_map/slice | solution.py:271
  4.2 0.0 copy-start
  4.2 1.6 %copy-done = bf16[256,2,2048]{2,1,0:T(2,128)(2,1)S(1)} copy-done((bf16[256,2,2048]{2,1,0:T(2,128)(2,1)S(1)}, bf16[256,2,2048]{2,1,0:T(2,128)(2,1)}, u32[]{:S(2)}) %copy-start) | copy-done | bytes 2097176
  5.8 0.0 copy-start.1
  5.8 0.7 %copy-done.1 = s32[16,32]{1,0:T(8,128)S(1)} copy-done((s32[16,32]{1,0:T(8,128)S(1)}, s32[16,32]{1,0:T(8,128)}, u32[]{:S(2)}) %copy-start.1) | copy-done | bytes 2072
  6.5 0.0 copy-start.2
  6.5 0.7 %copy-done.2 = bf16[2,8,32]{2,1,0:T(8,128)(2,1)S(1)} copy-done((bf16[2,8,32]{2,1,0:T(8,128)(2,1)S(1)}, bf16[2,8,32]{2,1,0:T(8,128)(2,1)}, u32[]{:S(2)}) %copy-start.2) | copy-done | bytes 1048
  7.2 0.0 copy-start.3
  7.2 0.7 %copy-done.3 = s32[256]{0:T(256)S(1)} copy-done((s32[256]{0:T(256)S(1)}, s32[256]{0:T(256)}, u32[]{:S(2)}) %copy-start.3) | copy-done | bytes 1048
  7.9 26.8 %shard_map.82 = (bf16[4,8,16,2048]{3,2,1,0:T(8,128)(2,1)S(1)}, bf16[512,512]{1,0:T(8,128)(2,1)S(1)}) custom-call(s32[256]{0:T(256)S(1)} %copy-done.3, bf16[256,32,128]{2,1,0:T(8,128)(2,1)S(1)} %bitcast.13, bf16[512,128]{1,0:T(8,128)(2,1)S(1)} %bitcast.16, bf16[512,128]{1,0:T(8,128)(2,1)S(1)} %bitcast.15, f32[16,256]{1,0:T(8,128)S(1)} %concatenate.3.params, ...), custom_call_target="tpu_custom_call" | custom-call | tf_op jit(solution)/shard_map/pallas_call | solution.py:284
  34.7 3.1 %shard_map.83 = bf16[512,2048]{1,0:T(8,128)(2,1)} custom-call(bf16[512,512]{1,0:T(8,128)(2,1)S(1)} %get-tuple-element.7.dense, bf16[512,2048]{1,0:T(8,128)(2,1)S(1)} %bitcast.14), custom_call_target="tpu_custom_call" | custom-call | tf_op jit(solution)/shard_map/pallas_call | solution.py:327
  (1 shorter events, 0.0 us)
Async XLA Ops:
  4.2 1.6 %copy-start = (bf16[256,2,2048]{2,1,0:T(2,128)(2,1)S(1)}, bf16[256,2,2048]{2,1,0:T(2,128)(2,1)}, u32[]{:S(2)}) copy-start(bf16[256,2,2048]{2,1,0:T(2,128)(2,1)} %param.8) | copy-start | bytes 6291460
  5.8 0.7 %copy-start.1 = (s32[16,32]{1,0:T(8,128)S(1)}, s32[16,32]{1,0:T(8,128)}, u32[]{:S(2)}) copy-start(s32[16,32]{1,0:T(8,128)} %footprint.1) | copy-start | bytes 6148
  6.5 0.7 %copy-start.2 = (bf16[2,8,32]{2,1,0:T(8,128)(2,1)S(1)}, bf16[2,8,32]{2,1,0:T(8,128)(2,1)}, u32[]{:S(2)}) copy-start(bf16[2,8,32]{2,1,0:T(8,128)(2,1)} %steering.1) | copy-start | bytes 3076
  7.2 0.7 %copy-start.3 = (s32[256]{0:T(256)S(1)}, s32[256]{0:T(256)}, u32[]{:S(2)}) copy-start(s32[256]{0:T(256)} %shifts.1) | copy-start | bytes 3076

commit v2 on v1

--- a/solution.py
+++ b/solution.py
@@ -22,10 +22,11 @@
 
 def beam_kernel(
     n_pulse, n_range, blocks, subs,
-    shifts, echoes, heads, tails, params, steering, footprint, tile_coeffs,
+    echoes_in, shifts_in, taps_in, angles_in, slopes_in, steering_in, footprint_in, coeffs_in, heads, tails,
     gathered, dense,
-    cells, left, right, left_f, right_f, rolled, y_re, y_im, taps_out, sent,
-    lhs_re, lhs_im, e_re, e_im, d_re, d_im, reach,
+    cells, shifts, shift_row, taps, angles, slopes, steering, footprint, coeffs,
+    left, right, left_f, right_f, rolled, y, taps_out, sent,
+    lhs, e_re, e_im, d_re, d_im, reach,
     load_sem, halo_send, halo_recv, own_sem,
     x_send, x_recv, sib_send, sib_recv, fwd_send, fwd_recv,
 ):
@@ -43,8 +44,16 @@
     def dev(p, z):
         return (gi, p, z)
 
-    load = pltpu.make_async_copy(echoes, cells, load_sem)
-    load.start()
+    loads = [
+        pltpu.make_async_copy(source, target, load_sem.at[n])
+        for n, (source, target) in enumerate([
+            (slopes_in, slopes), (taps_in, taps), (steering_in, steering), (angles_in, angles),
+            (shifts_in, shift_row), (shifts_in, shifts), (echoes_in, cells),
+            (footprint_in, footprint), (coeffs_in, coeffs),
+        ])
+    ]
+    for load in loads:
+        load.start()
 
     barrier = pltpu.get_barrier_semaphore()
     pl.semaphore_signal(barrier, inc=1, device_id=dev(sibling, zi), device_id_type=MESH_ID)
@@ -60,57 +69,62 @@
     def _():
         pl.semaphore_signal(barrier, inc=1, device_id=dev(me, zi + 1), device_id_type=MESH_ID)
 
-    pl.semaphore_wait(barrier, chips + jnp.minimum(zi, 1) + jnp.minimum(n_range - 1 - zi, 1))
-
-    def to_left():
-        return pltpu.make_async_remote_copy(
-            src_ref=heads, dst_ref=right, send_sem=halo_send.at[0], recv_sem=halo_recv.at[0],
-            device_id=dev(me, zi - 1), device_id_type=MESH_ID)
-
-    def to_right():
-        return pltpu.make_async_remote_copy(
-            src_ref=tails, dst_ref=left, send_sem=halo_send.at[1], recv_sem=halo_recv.at[1],
-            device_id=dev(me, zi + 1), device_id_type=MESH_ID)
-
-    @pl.when(has_left)
-    def _():
-        to_left().start()
-
-    @pl.when(has_right)
-    def _():
-        to_right().start()
-
-    lane = lax.broadcasted_iota(jnp.int32, (LANES, LANES), 1).astype(F32)
-    start = (zi * (blocks * LANES)).astype(F32)
-    for h in range(pulses // LANES):
-        span = pl.ds(h * LANES, LANES)
-
-        def column(row):
-            return jnp.transpose(jnp.broadcast_to(params[row:row + 1, span], (LANES, LANES)))
-
-        angle, slope, shift = column(TAPS), column(TAPS + 1), column(TAPS + 2)
-        phase = angle + slope * (start + lane)
-        e_re[span, :] = jnp.cos(phase)
-        e_im[span, :] = jnp.sin(phase)
-        step = slope * float(LANES)
-        d_re[span, :] = jnp.cos(step)
-        d_im[span, :] = jnp.sin(step)
-        reach[span, :] = shift + lane + float(LANES - TAPS // 2 + 1)
-
-    tap_phase = params[TAPS + 1:TAPS + 2, :] * lax.broadcasted_iota(jnp.int32, (TAPS, pulses), 0).astype(F32)
-    tap_re = params[0:TAPS, :] * jnp.cos(tap_phase)
-    tap_im = -params[0:TAPS, :] * jnp.sin(tap_phase)
-    st_re = steering[0].astype(F32)
-    st_im = steering[1].astype(F32)
+    for load in loads[:3]:
+        load.wait()
+    tap_phase = slopes[...] * lax.broadcasted_iota(jnp.int32, (TAPS, pulses), 0).astype(F32)
+    tap_re = taps[...] * jnp.cos(tap_phase)
+    tap_im = -taps[...] * jnp.sin(tap_phase)
+    weights = steering[...].astype(F32)
+    st_re, st_im = weights[0:BEAMS], weights[BEAMS:2 * BEAMS]
     for s in range(subs):
         g_re = tap_re[:, s * SUB:(s + 1) * SUB]
         g_im = tap_im[:, s * SUB:(s + 1) * SUB]
         for k in range(TAPS):
             w_re = st_re * g_re[k:k + 1] - st_im * g_im[k:k + 1]
             w_im = st_re * g_im[k:k + 1] + st_im * g_re[k:k + 1]
-            rows = pl.ds(k * 2 * BEAMS, 2 * BEAMS)
-            lhs_re[s, rows, :] = jnp.concatenate([w_re, w_im], axis=0).astype(BF16)
-            lhs_im[s, rows, :] = jnp.concatenate([-w_im, w_re], axis=0).astype(BF16)
+            both = jnp.concatenate(
+                [jnp.concatenate([w_re, -w_im], axis=1), jnp.concatenate([w_im, w_re], axis=1)], axis=0)
+            lhs[s, k * 2 * BEAMS:(k + 1) * 2 * BEAMS, :] = both.astype(BF16)
+
+    pl.semaphore_wait(barrier, chips + jnp.minimum(zi, 1) + jnp.minimum(n_range - 1 - zi, 1))
+
+    def to_left():
+        return pltpu.make_async_remote_copy(
+            src_ref=heads, dst_ref=right, send_sem=halo_send.at[0], recv_sem=halo_recv.at[0],
+            device_id=dev(me, zi - 1), device_id_type=MESH_ID)
+
+    def to_right():
+        return pltpu.make_async_remote_copy(
+            src_ref=tails, dst_ref=left, send_sem=halo_send.at[1], recv_sem=halo_recv.at[1],
+            device_id=dev(me, zi + 1), device_id_type=MESH_ID)
+
+    @pl.when(has_left)
+    def _():
+        to_left().start()
+
+    @pl.when(has_right)
+    def _():
+        to_right().start()
+
+    for load in loads[3:5]:
+        load.wait()
+    lane = lax.broadcasted_iota(jnp.int32, (LANES, LANES), 1).astype(F32)
+    start = (zi * (blocks * LANES)).astype(F32)
+    shift_values = shift_row[...].astype(F32)
+    step = slopes[...] * float(LANES)
+    step_re, step_im = jnp.cos(step), jnp.sin(step)
+    for h in range(pulses // LANES):
+        span = slice(h * LANES, (h + 1) * LANES)
+
+        def column(row):
+            return jnp.transpose(jnp.broadcast_to(row[:, span], (LANES, LANES)))
+
+        phase = column(angles[...]) + column(slopes[...]) * (start + lane)
+        e_re[span, :] = jnp.cos(phase)
+        e_im[span, :] = jnp.sin(phase)
+        d_re[span, :] = column(step_re)
+        d_im[span, :] = column(step_im)
+        reach[span, :] = column(shift_values) + lane + float(LANES - TAPS // 2 + 1)
 
     @pl.when(has_left)
     def _():
@@ -130,7 +144,8 @@
 
     left_f[...] = left[...].astype(F32)
     right_f[...] = right[...].astype(F32)
-    load.wait()
+    for load in loads[5:7]:
+        load.wait()
 
     def x_copy(d, s):
         peer = ((chip + d) % chips) * 2 + core
@@ -167,10 +182,10 @@
             for u in range(UNROLL):
                 j = group * UNROLL + u
                 pulse = s * SUB + j
-                amount = (LANES - (shifts[pulse] + (LANES - TAPS // 2 + 1))) & (LANES - 1)
-                rolled[0:own_rows, j, :] = pltpu.roll(cells[pulse].astype(F32), amount, axis=1)
-                rolled[own_rows:own_rows + 2, j, :] = pltpu.roll(left_f[pl.ds(2 * pulse, 2), :], amount, axis=1)
-                rolled[own_rows + 2:own_rows + 4, j, :] = pltpu.roll(right_f[pl.ds(2 * pulse, 2), :], amount, axis=1)
+                amount = (LANES - (shifts[0, pulse] + (LANES - TAPS // 2 + 1))) & (LANES - 1)
+                rolled[pl.ds(j, own_rows, SUB), :] = pltpu.roll(cells[pulse].astype(F32), amount, axis=1)
+                rolled[pl.ds(own_rows * SUB + j, 2, SUB), :] = pltpu.roll(left_f[pl.ds(2 * pulse, 2), :], amount, axis=1)
+                rolled[pl.ds((own_rows + 2) * SUB + j, 2, SUB), :] = pltpu.roll(right_f[pl.ds(2 * pulse, 2), :], amount, axis=1)
             return inner
 
         lax.fori_loop(0, SUB // UNROLL, some_pulses, 0)
@@ -185,7 +200,7 @@
         def block(b, c):
             b = min(b, blocks + 1)
             where = own_rows if b == 0 else own_rows + 2 if b == blocks + 1 else 2 * (b - 1)
-            return rolled[where + c]
+            return rolled[(where + c) * SUB:(where + c + 1) * SUB, :]
 
         for b in range(blocks + 1):
             z = [
@@ -193,12 +208,11 @@
                 for c in range(2)
             ]
             span = slice(b * LANES, (b + 1) * LANES)
-            y_re[:, span] = (now_re * z[0] - now_im * z[1]).astype(BF16)
-            y_im[:, span] = (now_im * z[0] + now_re * z[1]).astype(BF16)
+            y[0:SUB, span] = (now_re * z[0] - now_im * z[1]).astype(BF16)
+            y[SUB:2 * SUB, span] = (now_im * z[0] + now_re * z[1]).astype(BF16)
             now_re, now_im = now_re * turn_re - now_im * turn_im, now_im * turn_re + now_re * turn_im
 
-        taps_out[...] = jnp.dot(lhs_re[s], y_re[...], preferred_element_type=F32) + jnp.dot(
-            lhs_im[s], y_im[...], preferred_element_type=F32)
+        taps_out[...] = jnp.dot(lhs[s], y[...], preferred_element_type=F32)
         width = (blocks + 1) * LANES
         total = taps_out[0:2 * BEAMS, :]
         for k in range(1, TAPS):
@@ -223,12 +237,15 @@
     row = lax.broadcasted_iota(jnp.int32, (n_rows, FOOT), 0)
     beam = (row // (2 * BEAMS)) * BEAMS + row % BEAMS
     is_im = (row // BEAMS) % 2
+    for load in loads[7:]:
+        load.wait()
     for t in range(TILE_DEV):
         ids = footprint[pl.ds(me * TILE_DEV + t, 1), :]
         hit = beam == ids
         hot_re = jnp.where(hit & (is_im == 0), 1.0, 0.0).astype(BF16)
         hot_im = jnp.where(hit & (is_im == 1), 1.0, 0.0).astype(BF16)
-        c_re, c_im = tile_coeffs[t, 0], tile_coeffs[t, 1]
+        c_re = jnp.transpose(coeffs[t, 0].astype(F32)).astype(BF16)
+        c_im = jnp.transpose(coeffs[t, 1].astype(F32)).astype(BF16)
 
         def spread(a, b):
             return lax.dot_general(a, b, (((1,), (1,)), ((), ())), preferred_element_type=F32)
@@ -269,17 +286,11 @@
     by_block = echoes.reshape(pulses, 2, blocks, LANES).transpose(0, 2, 1, 3).reshape(pulses, 2 * blocks, LANES)
     heads = echoes[:, :, :LANES].reshape(2 * pulses, LANES)
     tails = echoes[:, :, width - LANES:].reshape(2 * pulses, LANES)
-    params = jnp.concatenate(
-        [
-            tap_weights.T, angles[None], slopes[None], shifts[None].astype(F32),
-            jnp.zeros((5, pulses), F32),
-        ],
-        axis=0,
-    )
     n_rows = n_pulse * subs * 2 * BEAMS
     out_rows = TILE_DEV * 2 * AZ
     vmem = pl.BlockSpec(memory_space=pltpu.VMEM)
-    hbm = pl.BlockSpec(memory_space=pl.ANY)
+    hbm = pl.BlockSpec(memory_space=pltpu.HBM)
+    anywhere = pl.BlockSpec(memory_space=pl.ANY)
     dma = pltpu.SemaphoreType.DMA
     gathered, dense = pl.pallas_call(
         functools.partial(beam_kernel, n_pulse, n_range, blocks, subs),
@@ -287,27 +298,33 @@
             jax.ShapeDtypeStruct((n_pulse, subs, 2 * BEAMS, width), BF16),
             jax.ShapeDtypeStruct((out_rows, n_rows), BF16),
         ),
-        in_specs=[pl.BlockSpec(memory_space=pltpu.SMEM), hbm, vmem, vmem, vmem, vmem, vmem, vmem],
-        out_specs=(hbm, vmem),
+        in_specs=[hbm] * 8 + [vmem] * 2,
+        out_specs=(anywhere, vmem),
         scratch_shapes=[
             pltpu.VMEM((pulses, 2 * blocks, LANES), BF16),
+            pltpu.SMEM((1, pulses), jnp.int32),
+            pltpu.VMEM((1, pulses), jnp.int32),
+            pltpu.VMEM((TAPS, pulses), F32),
+            pltpu.VMEM((1, pulses), F32),
+            pltpu.VMEM((1, pulses), F32),
+            pltpu.VMEM((2 * BEAMS, SUB), BF16),
+            pltpu.VMEM(footprint.shape, jnp.int32),
+            pltpu.VMEM((TILE_DEV, 2, FOOT, AZ), BF16),
             pltpu.VMEM((2 * pulses, LANES), BF16),
             pltpu.VMEM((2 * pulses, LANES), BF16),
             pltpu.VMEM((2 * pulses, LANES), F32),
             pltpu.VMEM((2 * pulses, LANES), F32),
-            pltpu.VMEM((2 * blocks + 4, SUB, LANES), F32),
-            pltpu.VMEM((SUB, width + LANES), BF16),
-            pltpu.VMEM((SUB, width + LANES), BF16),
+            pltpu.VMEM(((2 * blocks + 4) * SUB, LANES), F32),
+            pltpu.VMEM((2 * SUB, width + LANES), BF16),
             pltpu.VMEM((TAPS * 2 * BEAMS, width + LANES), F32),
             pltpu.VMEM((subs, 2 * BEAMS, width), BF16),
-            pltpu.VMEM((subs, TAPS * 2 * BEAMS, SUB), BF16),
-            pltpu.VMEM((subs, TAPS * 2 * BEAMS, SUB), BF16),
-            pltpu.VMEM((pulses, LANES), F32),
-            pltpu.VMEM((pulses, LANES), F32),
-            pltpu.VMEM((pulses, LANES), F32),
-            pltpu.VMEM((pulses, LANES), F32),
-            pltpu.VMEM((pulses, LANES), F32),
-            dma(()),
+            pltpu.VMEM((subs, TAPS * 2 * BEAMS, 2 * SUB), BF16),
+            pltpu.VMEM((pulses, LANES), F32),
+            pltpu.VMEM((pulses, LANES), F32),
+            pltpu.VMEM((pulses, LANES), F32),
+            pltpu.VMEM((pulses, LANES), F32),
+            pltpu.VMEM((pulses, LANES), F32),
+            dma((9,)),
             dma((2,)),
             dma((2,)),
             dma((subs,)),
@@ -319,9 +336,12 @@
             dma((chips - 1, subs)),
         ],
         compiler_params=pltpu.CompilerParams(
-            collective_id=0, has_side_effects=True, vmem_limit_bytes=48 * 1024 * 1024
+            collective_id=0, has_side_effects=True, vmem_limit_bytes=63 * 1024 * 1024
         ),
-    )(shifts, by_block, heads, tails, params, steering, footprint, tile_coeffs)
+    )(
+        by_block, shifts[None], tap_weights.T, angles[None], slopes[None], steering.reshape(2 * BEAMS, SUB),
+        footprint, tile_coeffs.transpose(0, 1, 3, 2), heads, tails,
+    )
 
     columns = 512
     image = pl.pallas_call(
@@ -333,7 +353,7 @@
             pl.BlockSpec((n_rows, columns), lambda i: (0, i)),
         ],
         out_specs=pl.BlockSpec((out_rows, columns), lambda i: (0, i)),
-        compiler_params=pltpu.CompilerParams(vmem_limit_bytes=48 * 1024 * 1024),
+        compiler_params=pltpu.CompilerParams(vmem_limit_bytes=63 * 1024 * 1024),
     )(dense, gathered.reshape(n_rows, width))
     return image.reshape(TILE_DEV, 2, AZ, width)
 

time: 38.2 us -> 35.1 us (0.919)
  local copies, waits for them, and re-layouts: 7.18 us -> 1.85 us
  Pallas kernels: 29.9 us -> 32.9 us
  other arithmetic: 0.68 us -> 0 us
    unnamed x9 -> x0, local copies, waits for them, and re-layouts: 4.6 us -> none
    pallas_call x1, Pallas kernels: 3.06 us -> 4.76 us  [body(): pl.pallas_call(project_kernel, grid=(width // columns,), out_shape=jax.Sh...]
    concatenate x1 -> x0, local copies, waits for them, and re-layouts: 1.41 us -> none  [body(): jnp.concatenate([tap_weights.T, angles[None], slopes[None], shifts[None]....]
    pallas_call x1, Pallas kernels: 26.8 us -> 28.1 us  [body(): pl.pallas_call(functools.partial(beam_kernel, n_pulse, n_range, blocks, s...]
    convert_element_type x1 -> x0, other arithmetic: 0.68 us -> none  [body(): shifts[None].astype(F32)]
    slice x1, local copies, waits for them, and re-layouts: 1.17 us -> 1.85 us  [body(): tails = echoes[:, :, width - LANES:].reshape(2 * pulses, LANES)]
where the time goes in v2:
time: 35.1 us; the launch traced here: 34.8 us
  Pallas kernels  32.9 us (94%)
  local copies, waits for them, and re-layouts  1.85 us (5%)
    pallas_call x1, Pallas kernels, body(): pl.pallas_call(functools.partial(beam_kernel, n_pulse, n_range, blocks, s...  28.1 us
    pallas_call x1, Pallas kernels, body(): pl.pallas_call(project_kernel, grid=(width // columns,), out_shape=jax.Sh...  4.76 us
    slice x1, local copies, waits for them, and re-layouts, body(): tails = echoes[:, :, width - LANES:].reshape(2 * pulses, LANES)  1.85 us

profile of v2, /device:TPU:1, one launch (start us, length us, event | category | flops | bytes accessed | tf_op | source)
XLA Modules:
  0.0 34.8 jit_solution(11051879155640820863)
XLA Ops:
  0.0 1.9 %fusion = (bf16[256,2,128]{2,1,0:T(2,128)(2,1)}, bf16[256,2,128]{2,1,0:T(2,128)(2,1)}) fusion(bf16[256,2,2048]{2,1,0:T(2,128)(2,1)} %param.8), kind=kLoop, calls=%fused_computation | loop fusion | bytes 524288 | tf_op jit(solution)/shard_map/slice | solution.py:288
  1.9 28.1 %shard_map.82 = (bf16[4,8,16,2048]{3,2,1,0:T(8,128)(2,1)}, bf16[512,512]{1,0:T(8,128)(2,1)}) custom-call(bf16[256,32,128]{2,1,0:T(8,128)(2,1)} %bitcast.15, s32[1,256]{1,0:T(1,128)} %bitcast.22, f32[8,256]{1,0:T(8,128)} %bitcast.20, f32[1,256]{1,0:T(1,128)} %bitcast.23, f32[1,256]{1,0:T(1,128)} %bitcast.24, bf16[16,32]{1,0:T(8,128)(2,1)} %bitcast.21, ...), custom_call_target="tpu_custom_call" | custom-call | tf_op jit(solution)/shard_map/pallas_call | solution.py:295
  30.0 4.8 %shard_map.83 = bf16[512,2048]{1,0:T(8,128)(2,1)} custom-call(bf16[512,512]{1,0:T(8,128)(2,1)} %get-tuple-element.7.dense, bf16[512,2048]{1,0:T(8,128)(2,1)} %bitcast.16), custom_call_target="tpu_custom_call" | custom-call | tf_op jit(solution)/shard_map/pallas_call | solution.py:347

commit v3 on v2

--- a/solution.py
+++ b/solution.py
@@ -69,42 +69,49 @@
     def _():
         pl.semaphore_signal(barrier, inc=1, device_id=dev(me, zi + 1), device_id_type=MESH_ID)
 
+    pl.semaphore_wait(barrier, chips + jnp.minimum(zi, 1) + jnp.minimum(n_range - 1 - zi, 1))
+
+    def to_left():
+        return pltpu.make_async_remote_copy(
+            src_ref=heads, dst_ref=right, send_sem=halo_send.at[0], recv_sem=halo_recv.at[0],
+            device_id=dev(me, zi - 1), device_id_type=MESH_ID)
+
+    def to_right():
+        return pltpu.make_async_remote_copy(
+            src_ref=tails, dst_ref=left, send_sem=halo_send.at[1], recv_sem=halo_recv.at[1],
+            device_id=dev(me, zi + 1), device_id_type=MESH_ID)
+
+    @pl.when(has_left)
+    def _():
+        to_left().start()
+
+    @pl.when(has_right)
+    def _():
+        to_right().start()
+
     for load in loads[:3]:
         load.wait()
     tap_phase = slopes[...] * lax.broadcasted_iota(jnp.int32, (TAPS, pulses), 0).astype(F32)
     tap_re = taps[...] * jnp.cos(tap_phase)
     tap_im = -taps[...] * jnp.sin(tap_phase)
     weights = steering[...].astype(F32)
-    st_re, st_im = weights[0:BEAMS], weights[BEAMS:2 * BEAMS]
+    st_re = jnp.concatenate([weights[0:BEAMS]] * subs, axis=1)
+    st_im = jnp.concatenate([weights[BEAMS:2 * BEAMS]] * subs, axis=1)
+    from_re, from_im = [], []
+    for k in range(TAPS):
+        w_re = st_re * tap_re[k:k + 1] - st_im * tap_im[k:k + 1]
+        w_im = st_re * tap_im[k:k + 1] + st_im * tap_re[k:k + 1]
+        from_re += [w_re, w_im]
+        from_im += [-w_im, w_re]
+    from_re = jnp.concatenate(from_re, axis=0)
+    from_im = jnp.concatenate(from_im, axis=0)
+    on_re = lax.broadcasted_iota(jnp.int32, (TAPS * 2 * BEAMS, LANES), 1) < SUB
     for s in range(subs):
-        g_re = tap_re[:, s * SUB:(s + 1) * SUB]
-        g_im = tap_im[:, s * SUB:(s + 1) * SUB]
-        for k in range(TAPS):
-            w_re = st_re * g_re[k:k + 1] - st_im * g_im[k:k + 1]
-            w_im = st_re * g_im[k:k + 1] + st_im * g_re[k:k + 1]
-            both = jnp.concatenate(
-                [jnp.concatenate([w_re, -w_im], axis=1), jnp.concatenate([w_im, w_re], axis=1)], axis=0)
-            lhs[s, k * 2 * BEAMS:(k + 1) * 2 * BEAMS, :] = both.astype(BF16)
-
-    pl.semaphore_wait(barrier, chips + jnp.minimum(zi, 1) + jnp.minimum(n_range - 1 - zi, 1))
-
-    def to_left():
-        return pltpu.make_async_remote_copy(
-            src_ref=heads, dst_ref=right, send_sem=halo_send.at[0], recv_sem=halo_recv.at[0],
-            device_id=dev(me, zi - 1), device_id_type=MESH_ID)
-
-    def to_right():
-        return pltpu.make_async_remote_copy(
-            src_ref=tails, dst_ref=left, send_sem=halo_send.at[1], recv_sem=halo_recv.at[1],
-            device_id=dev(me, zi + 1), device_id_type=MESH_ID)
-
-    @pl.when(has_left)
-    def _():
-        to_left().start()
-
-    @pl.when(has_right)
-    def _():
-        to_right().start()
+        first = s * SUB // LANES * LANES
+        off = s * SUB - first
+        part_re = pltpu.roll(from_re[:, first:first + LANES], (LANES - off) % LANES, axis=1)
+        part_im = pltpu.roll(from_im[:, first:first + LANES], (LANES + SUB - off) % LANES, axis=1)
+        lhs[s] = jnp.where(on_re, part_re, part_im)[:, :2 * SUB].astype(BF16)
 
     for load in loads[3:5]:
         load.wait()
@@ -179,13 +186,21 @@
 
     def one_sub(s, carry):
         def some_pulses(group, inner):
+            turned = []
+            for u in range(UNROLL):
+                pulse = s * SUB + group * UNROLL + u
+                amount = (LANES - (shifts[0, pulse] + (LANES - TAPS // 2 + 1))) & (LANES - 1)
+                turned.append([
+                    pltpu.roll(part, amount, axis=1)
+                    for part in (
+                        cells[pulse].astype(F32), left_f[pl.ds(2 * pulse, 2), :], right_f[pl.ds(2 * pulse, 2), :],
+                    )
+                ])
             for u in range(UNROLL):
                 j = group * UNROLL + u
-                pulse = s * SUB + j
-                amount = (LANES - (shifts[0, pulse] + (LANES - TAPS // 2 + 1))) & (LANES - 1)
-                rolled[pl.ds(j, own_rows, SUB), :] = pltpu.roll(cells[pulse].astype(F32), amount, axis=1)
-                rolled[pl.ds(own_rows * SUB + j, 2, SUB), :] = pltpu.roll(left_f[pl.ds(2 * pulse, 2), :], amount, axis=1)
-                rolled[pl.ds((own_rows + 2) * SUB + j, 2, SUB), :] = pltpu.roll(right_f[pl.ds(2 * pulse, 2), :], amount, axis=1)
+                rolled[pl.ds(j, own_rows, SUB), :] = turned[u][0]
+                rolled[pl.ds(own_rows * SUB + j, 2, SUB), :] = turned[u][1]
+                rolled[pl.ds((own_rows + 2) * SUB + j, 2, SUB), :] = turned[u][2]
             return inner
 
         lax.fori_loop(0, SUB // UNROLL, some_pulses, 0)

time: 35.1 us -> 35.1 us (level)
  no operation moved by 1% of the time
where the time goes in v3:
time: 35.1 us; the launch traced here: 34.7 us
  Pallas kernels  32.9 us (94%)
  local copies, waits for them, and re-layouts  1.85 us (5%)
    pallas_call x1, Pallas kernels, body(): pl.pallas_call(functools.partial(beam_kernel, n_pulse, n_range, blocks, s...  28.1 us
    pallas_call x1, Pallas kernels, body(): pl.pallas_call(project_kernel, grid=(width // columns,), out_shape=jax.Sh...  4.76 us
    slice x1, local copies, waits for them, and re-layouts, body(): tails = echoes[:, :, width - LANES:].reshape(2 * pulses, LANES)  1.85 us

profile of v3, /device:TPU:1, one launch (start us, length us, event | category | flops | bytes accessed | tf_op | source)
XLA Modules:
  0.0 34.7 jit_solution(3657807646804568557)
XLA Ops:
  0.0 1.9 %fusion = (bf16[256,2,128]{2,1,0:T(2,128)(2,1)}, bf16[256,2,128]{2,1,0:T(2,128)(2,1)}) fusion(bf16[256,2,2048]{2,1,0:T(2,128)(2,1)} %param.8), kind=kLoop, calls=%fused_computation | loop fusion | bytes 524288 | tf_op jit(solution)/shard_map/slice | solution.py:303
  1.9 28.1 %shard_map.82 = (bf16[4,8,16,2048]{3,2,1,0:T(8,128)(2,1)}, bf16[512,512]{1,0:T(8,128)(2,1)}) custom-call(bf16[256,32,128]{2,1,0:T(8,128)(2,1)} %bitcast.15, s32[1,256]{1,0:T(1,128)} %bitcast.22, f32[8,256]{1,0:T(8,128)} %bitcast.20, f32[1,256]{1,0:T(1,128)} %bitcast.23, f32[1,256]{1,0:T(1,128)} %bitcast.24, bf16[16,32]{1,0:T(8,128)(2,1)} %bitcast.21, ...), custom_call_target="tpu_custom_call" | custom-call | tf_op jit(solution)/shard_map/pallas_call | solution.py:310
  30.0 4.8 %shard_map.83 = bf16[512,2048]{1,0:T(8,128)(2,1)} custom-call(bf16[512,512]{1,0:T(8,128)(2,1)} %get-tuple-element.7.dense, bf16[512,2048]{1,0:T(8,128)(2,1)} %bitcast.16), custom_call_target="tpu_custom_call" | custom-call | tf_op jit(solution)/shard_map/pallas_call | solution.py:362

commit v4 on v3

--- a/solution.py
+++ b/solution.py
@@ -18,6 +18,7 @@
 BF16 = jnp.bfloat16
 MESH_ID = pl.DeviceIdType.MESH
 UNROLL = 8
+LAG = 4
 
 
 def beam_kernel(
@@ -239,14 +240,15 @@
         sib_copy(s).start()
         own_copy(s).start()
 
-        @pl.when(s >= 2)
+        @pl.when(s >= LAG)
         def _():
-            forward(s - 2)
+            forward(s - LAG)
 
         return carry
 
     lax.fori_loop(0, subs, one_sub, 0)
-    forward(subs - 2)
+    for s in range(subs - LAG, subs - 1):
+        forward(s)
 
     n_rows = n_pulse * subs * 2 * BEAMS
     row = lax.broadcasted_iota(jnp.int32, (n_rows, FOOT), 0)

time: 35.1 us -> 33.3 us (0.949)
  Pallas kernels: 32.9 us -> 31.1 us
    pallas_call x1, Pallas kernels: 28.1 us -> 26.4 us  [body(): pl.pallas_call(functools.partial(beam_kernel, n_pulse, n_range, blocks, s...]
where the time goes in v4:
time: 33.3 us; the launch traced here: 33 us
  Pallas kernels  31.1 us (93%)
  local copies, waits for them, and re-layouts  1.85 us (6%)
    pallas_call x1, Pallas kernels, body(): pl.pallas_call(functools.partial(beam_kernel, n_pulse, n_range, blocks, s...  26.4 us
    pallas_call x1, Pallas kernels, body(): pl.pallas_call(project_kernel, grid=(width // columns,), out_shape=jax.Sh...  4.76 us
    slice x1, local copies, waits for them, and re-layouts, body(): tails = echoes[:, :, width - LANES:].reshape(2 * pulses, LANES)  1.85 us

profile of v4, /device:TPU:1, one launch (start us, length us, event | category | flops | bytes accessed | tf_op | source)
XLA Modules:
  0.0 33.0 jit_solution(11625103397174508933)
XLA Ops:
  0.0 1.9 %fusion = (bf16[256,2,128]{2,1,0:T(2,128)(2,1)}, bf16[256,2,128]{2,1,0:T(2,128)(2,1)}) fusion(bf16[256,2,2048]{2,1,0:T(2,128)(2,1)} %param.8), kind=kLoop, calls=%fused_computation | loop fusion | bytes 524288 | tf_op jit(solution)/shard_map/slice | solution.py:305
  1.9 26.4 %shard_map.82 = (bf16[4,8,16,2048]{3,2,1,0:T(8,128)(2,1)}, bf16[512,512]{1,0:T(8,128)(2,1)}) custom-call(bf16[256,32,128]{2,1,0:T(8,128)(2,1)} %bitcast.15, s32[1,256]{1,0:T(1,128)} %bitcast.22, f32[8,256]{1,0:T(8,128)} %bitcast.20, f32[1,256]{1,0:T(1,128)} %bitcast.23, f32[1,256]{1,0:T(1,128)} %bitcast.24, bf16[16,32]{1,0:T(8,128)(2,1)} %bitcast.21, ...), custom_call_target="tpu_custom_call" | custom-call | tf_op jit(solution)/shard_map/pallas_call | solution.py:312
  28.2 4.8 %shard_map.83 = bf16[512,2048]{1,0:T(8,128)(2,1)} custom-call(bf16[512,512]{1,0:T(8,128)(2,1)} %get-tuple-element.7.dense, bf16[512,2048]{1,0:T(8,128)(2,1)} %bitcast.16), custom_call_target="tpu_custom_call" | custom-call | tf_op jit(solution)/shard_map/pallas_call | solution.py:364

commit v5 on v4

--- a/solution.py
+++ b/solution.py
@@ -19,16 +19,17 @@
 MESH_ID = pl.DeviceIdType.MESH
 UNROLL = 8
 LAG = 4
+COLUMNS = 256
 
 
 def beam_kernel(
     n_pulse, n_range, blocks, subs,
     echoes_in, shifts_in, taps_in, angles_in, slopes_in, steering_in, footprint_in, coeffs_in, heads, tails,
-    gathered, dense,
+    out,
     cells, shifts, shift_row, taps, angles, slopes, steering, footprint, coeffs,
-    left, right, left_f, right_f, rolled, y, taps_out, sent,
+    left, right, left_f, right_f, rolled, y, taps_out, gathered, dense, half_sum, image,
     lhs, e_re, e_im, d_re, d_im, reach,
-    load_sem, halo_send, halo_recv, own_sem,
+    load_sem, halo_send, halo_recv, out_sem,
     x_send, x_recv, sib_send, sib_recv, fwd_send, fwd_recv,
 ):
     chips = n_pulse // 2
@@ -155,28 +156,28 @@
     for load in loads[5:7]:
         load.wait()
 
+    def slot(s, owner):
+        return gathered.at[pl.ds(pl.multiple_of((s * n_pulse + owner) * 2 * BEAMS, 2 * BEAMS), 2 * BEAMS), :]
+
     def x_copy(d, s):
         peer = ((chip + d) % chips) * 2 + core
         return pltpu.make_async_remote_copy(
-            src_ref=sent.at[s], dst_ref=gathered.at[me, s],
+            src_ref=slot(s, me), dst_ref=slot(s, me),
             send_sem=x_send.at[d - 1, s], recv_sem=x_recv.at[d - 1, s],
             device_id=dev(peer, zi), device_id_type=MESH_ID)
 
     def sib_copy(s):
         return pltpu.make_async_remote_copy(
-            src_ref=sent.at[s], dst_ref=gathered.at[me, s],
+            src_ref=slot(s, me), dst_ref=slot(s, me),
             send_sem=sib_send.at[s], recv_sem=sib_recv.at[s],
             device_id=dev(sibling, zi), device_id_type=MESH_ID)
 
     def fwd_copy(d, s):
         owner = ((chip + chips - d) % chips) * 2 + core
         return pltpu.make_async_remote_copy(
-            src_ref=gathered.at[owner, s], dst_ref=gathered.at[owner, s],
+            src_ref=slot(s, owner), dst_ref=slot(s, owner),
             send_sem=fwd_send.at[d - 1, s], recv_sem=fwd_recv.at[d - 1, s],
             device_id=dev(sibling, zi), device_id_type=MESH_ID)
-
-    def own_copy(s):
-        return pltpu.make_async_copy(sent.at[s], gathered.at[me, s], own_sem.at[s])
 
     def forward(s):
         for d in range(1, chips):
@@ -233,12 +234,11 @@
         total = taps_out[0:2 * BEAMS, :]
         for k in range(1, TAPS):
             total = total + pltpu.roll(taps_out[k * 2 * BEAMS:(k + 1) * 2 * BEAMS, :], width - k, axis=1)
-        sent[s] = total[:, :blocks * LANES].astype(BF16)
+        slot(s, me)[...] = total[:, :blocks * LANES].astype(BF16)
 
         for d in range(1, chips):
             x_copy(d, s).start()
         sib_copy(s).start()
-        own_copy(s).start()
 
         @pl.when(s >= LAG)
         def _():
@@ -247,12 +247,10 @@
         return carry
 
     lax.fori_loop(0, subs, one_sub, 0)
-    for s in range(subs - LAG, subs - 1):
-        forward(s)
-
     n_rows = n_pulse * subs * 2 * BEAMS
     row = lax.broadcasted_iota(jnp.int32, (n_rows, FOOT), 0)
-    beam = (row // (2 * BEAMS)) * BEAMS + row % BEAMS
+    block_row = row // (2 * BEAMS)
+    beam = ((block_row % n_pulse) * subs + block_row // n_pulse) * BEAMS + row % BEAMS
     is_im = (row // BEAMS) % 2
     for load in loads[7:]:
         load.wait()
@@ -270,18 +268,61 @@
         dense[t * 2 * AZ:t * 2 * AZ + AZ, :] = (spread(c_re, hot_re) - spread(c_im, hot_im)).astype(BF16)
         dense[t * 2 * AZ + AZ:(t + 1) * 2 * AZ, :] = (spread(c_im, hot_re) + spread(c_re, hot_im)).astype(BF16)
 
-    forward(subs - 1)
+    def landed(first, last):
+        def one(s, carry):
+            sib_copy(s).wait_recv()
+            for d in range(1, chips):
+                fwd_copy(d, s).wait_recv()
+            return carry
+
+        lax.fori_loop(first, last, one, 0)
+
+    early = subs - LAG
+    half = early * n_pulse * 2 * BEAMS
+    pieces = blocks * LANES // COLUMNS
+
+    def columns(n):
+        return pl.ds(pl.multiple_of(n * COLUMNS, COLUMNS), COLUMNS)
+
+    def first_half(n, carry):
+        half_sum[:, columns(n)] = jnp.dot(
+            dense[:, 0:half], gathered[0:half, columns(n)], preferred_element_type=F32)
+        return carry
+
+    def out_copy(n):
+        return pltpu.make_async_copy(image.at[:, columns(n)], out.at[:, columns(n)], out_sem.at[n])
+
+    def second_half(n, carry):
+        image[:, columns(n)] = (half_sum[:, columns(n)] + jnp.dot(
+            dense[:, half:n_rows], gathered[half:n_rows, columns(n)], preferred_element_type=F32)).astype(BF16)
+        out_copy(n).start()
+        return carry
+
+    forward(early)
+    landed(0, early)
+    lax.fori_loop(0, pieces // 2, first_half, 0)
+    forward(early + 1)
+    lax.fori_loop(pieces // 2, pieces, first_half, 0)
+    for s in range(early + 2, subs):
+        forward(s)
+    landed(early, subs)
+    lax.fori_loop(0, pieces, second_half, 0)
 
     def finish(s, carry):
-        own_copy(s).wait()
-        sib_copy(s).wait()
+        sib_copy(s).wait_send()
         for d in range(1, chips):
             x_copy(d, s).wait_send()
-            fwd_copy(d, s).wait()
+            fwd_copy(d, s).wait_send()
         return carry
 
     lax.fori_loop(0, subs, finish, 0)
 
+    def drain(n, carry):
+        out_copy(n).wait()
+        return carry
+
+    lax.fori_loop(0, pieces, drain, 0)
+
     @pl.when(has_left)
     def _():
         to_left().wait_send()
@@ -289,10 +330,6 @@
     @pl.when(has_right)
     def _():
         to_right().wait_send()
-
-
-def project_kernel(dense, beams, out):
-    out[...] = jnp.dot(dense[...], beams[...], preferred_element_type=F32).astype(BF16)
 
 
 def body(n_pulse, n_range, echoes, shifts, tap_weights, angles, slopes, steering, footprint, tile_coeffs):
@@ -307,16 +344,12 @@
     out_rows = TILE_DEV * 2 * AZ
     vmem = pl.BlockSpec(memory_space=pltpu.VMEM)
     hbm = pl.BlockSpec(memory_space=pltpu.HBM)
-    anywhere = pl.BlockSpec(memory_space=pl.ANY)
     dma = pltpu.SemaphoreType.DMA
-    gathered, dense = pl.pallas_call(
+    image = pl.pallas_call(
         functools.partial(beam_kernel, n_pulse, n_range, blocks, subs),
-        out_shape=(
-            jax.ShapeDtypeStruct((n_pulse, subs, 2 * BEAMS, width), BF16),
-            jax.ShapeDtypeStruct((out_rows, n_rows), BF16),
-        ),
+        out_shape=jax.ShapeDtypeStruct((out_rows, width), BF16),
         in_specs=[hbm] * 8 + [vmem] * 2,
-        out_specs=(anywhere, vmem),
+        out_specs=hbm,
         scratch_shapes=[
             pltpu.VMEM((pulses, 2 * blocks, LANES), BF16),
             pltpu.SMEM((1, pulses), jnp.int32),
@@ -334,7 +367,10 @@
             pltpu.VMEM(((2 * blocks + 4) * SUB, LANES), F32),
             pltpu.VMEM((2 * SUB, width + LANES), BF16),
             pltpu.VMEM((TAPS * 2 * BEAMS, width + LANES), F32),
-            pltpu.VMEM((subs, 2 * BEAMS, width), BF16),
+            pltpu.VMEM((n_rows, width), BF16),
+            pltpu.VMEM((out_rows, n_rows), BF16),
+            pltpu.VMEM((out_rows, width), F32),
+            pltpu.VMEM((out_rows, width), BF16),
             pltpu.VMEM((subs, TAPS * 2 * BEAMS, 2 * SUB), BF16),
             pltpu.VMEM((pulses, LANES), F32),
             pltpu.VMEM((pulses, LANES), F32),
@@ -344,7 +380,7 @@
             dma((9,)),
             dma((2,)),
             dma((2,)),
-            dma((subs,)),
+            dma((width // COLUMNS,)),
             dma((chips - 1, subs)),
             dma((chips - 1, subs)),
             dma((subs,)),
@@ -359,19 +395,6 @@
         by_block, shifts[None], tap_weights.T, angles[None], slopes[None], steering.reshape(2 * BEAMS, SUB),
         footprint, tile_coeffs.transpose(0, 1, 3, 2), heads, tails,
     )
-
-    columns = 512
-    image = pl.pallas_call(
-        project_kernel,
-        grid=(width // columns,),
-        out_shape=jax.ShapeDtypeStruct((out_rows, width), BF16),
-        in_specs=[
-            pl.BlockSpec((out_rows, n_rows), lambda i: (0, 0)),
-            pl.BlockSpec((n_rows, columns), lambda i: (0, i)),
-        ],
-        out_specs=pl.BlockSpec((out_rows, columns), lambda i: (0, i)),
-        compiler_params=pltpu.CompilerParams(vmem_limit_bytes=63 * 1024 * 1024),
-    )(dense, gathered.reshape(n_rows, width))
     return image.reshape(TILE_DEV, 2, AZ, width)
 
 

time: 33.3 us -> 32.9 us (0.988)
  Pallas kernels: 31.1 us -> 27.7 us
  local copies, waits for them, and re-layouts: 1.85 us -> 5.03 us
    pallas_call x1 -> x0, Pallas kernels: 4.76 us -> none  [body(): pl.pallas_call(project_kernel, grid=(width // columns,), out_shape=jax.Sh...]
    unnamed x0 -> x1, local copies, waits for them, and re-layouts: none -> 3.16 us
    pallas_call x1, Pallas kernels: 26.4 us -> 27.7 us  [body(): pl.pallas_call(functools.partial(beam_kernel, n_pulse, n_range, blocks, s...]
where the time goes in v5:
time: 32.9 us; the launch traced here: 32.8 us
  Pallas kernels  27.7 us (84%)
  local copies, waits for them, and re-layouts  5.03 us (15%)
    pallas_call x1, Pallas kernels, body(): pl.pallas_call(functools.partial(beam_kernel, n_pulse, n_range, blocks, s...  27.7 us
    unnamed x1, local copies, waits for them, and re-layouts  3.16 us
    slice x1, local copies, waits for them, and re-layouts, body(): tails = echoes[:, :, width - LANES:].reshape(2 * pulses, LANES)  1.88 us

profile of v5, /device:TPU:1, one launch (start us, length us, event | category | flops | bytes accessed | tf_op | source)
XLA Modules:
  0.0 32.8 jit_solution(7464709841595091637)
XLA Ops:
  0.0 1.9 %fusion = (bf16[256,2,128]{2,1,0:T(2,128)(2,1)}, bf16[256,2,128]{2,1,0:T(2,128)(2,1)}) fusion(bf16[256,2,2048]{2,1,0:T(2,128)(2,1)} %param.8), kind=kLoop, calls=%fused_computation | loop fusion | bytes 524288 | tf_op jit(solution)/shard_map/slice | solution.py:342
  1.9 27.7 %shard_map.82 = bf16[512,2048]{1,0:T(8,128)(2,1)} custom-call(bf16[256,32,128]{2,1,0:T(8,128)(2,1)} %bitcast.15, s32[1,256]{1,0:T(1,128)} %bitcast.21, f32[8,256]{1,0:T(8,128)} %bitcast.19, f32[1,256]{1,0:T(1,128)} %bitcast.22, f32[1,256]{1,0:T(1,128)} %bitcast.23, bf16[16,32]{1,0:T(8,128)(2,1)} %bitcast.20, s32[16,32]{1,0:T(8,128)} %footprint_in.1, ...), custom_call_target="tpu_custom_call" | custom-call | tf_op jit(solution)/shard_map/pallas_call | solution.py:348
  29.6 3.2 %copy.11 = bf16[4,2,64,2048]{3,2,1,0:T(8,128)(2,1)} copy(bf16[4,2,64,2048]{3,2,1,0:T(8,128)(2,1)} %bitcast.14) | data formatting | bytes 4194304

commit v6 on v5

--- a/solution.py
+++ b/solution.py
@@ -19,6 +19,8 @@
 MESH_ID = pl.DeviceIdType.MESH
 UNROLL = 8
 LAG = 4
+PITCH = SUB + 8
+COPIES = 8
 COLUMNS = 256
 
 
@@ -200,9 +202,9 @@
                 ])
             for u in range(UNROLL):
                 j = group * UNROLL + u
-                rolled[pl.ds(j, own_rows, SUB), :] = turned[u][0]
-                rolled[pl.ds(own_rows * SUB + j, 2, SUB), :] = turned[u][1]
-                rolled[pl.ds((own_rows + 2) * SUB + j, 2, SUB), :] = turned[u][2]
+                rolled[pl.ds(j, own_rows, PITCH), :] = turned[u][0]
+                rolled[pl.ds(own_rows * PITCH + j, 2, PITCH), :] = turned[u][1]
+                rolled[pl.ds((own_rows + 2) * PITCH + j, 2, PITCH), :] = turned[u][2]
             return inner
 
         lax.fori_loop(0, SUB // UNROLL, some_pulses, 0)
@@ -217,7 +219,7 @@
         def block(b, c):
             b = min(b, blocks + 1)
             where = own_rows if b == 0 else own_rows + 2 if b == blocks + 1 else 2 * (b - 1)
-            return rolled[(where + c) * SUB:(where + c + 1) * SUB, :]
+            return rolled[(where + c) * PITCH:(where + c) * PITCH + SUB, :]
 
         for b in range(blocks + 1):
             z = [
@@ -330,6 +332,18 @@
     @pl.when(has_right)
     def _():
         to_right().wait_send()
+
+
+def hand_out(image, out, sems):
+    rows = image.shape[0] // COPIES
+    copies = [
+        pltpu.make_async_copy(image.at[n * rows:(n + 1) * rows], out.at[n * rows:(n + 1) * rows], sems.at[n])
+        for n in range(COPIES)
+    ]
+    for copy in copies:
+        copy.start()
+    for copy in copies:
+        copy.wait()
 
 
 def body(n_pulse, n_range, echoes, shifts, tap_weights, angles, slopes, steering, footprint, tile_coeffs):
@@ -364,7 +378,7 @@
             pltpu.VMEM((2 * pulses, LANES), BF16),
             pltpu.VMEM((2 * pulses, LANES), F32),
             pltpu.VMEM((2 * pulses, LANES), F32),
-            pltpu.VMEM(((2 * blocks + 4) * SUB, LANES), F32),
+            pltpu.VMEM(((2 * blocks + 4) * PITCH, LANES), F32),
             pltpu.VMEM((2 * SUB, width + LANES), BF16),
             pltpu.VMEM((TAPS * 2 * BEAMS, width + LANES), F32),
             pltpu.VMEM((n_rows, width), BF16),
@@ -395,6 +409,14 @@
         by_block, shifts[None], tap_weights.T, angles[None], slopes[None], steering.reshape(2 * BEAMS, SUB),
         footprint, tile_coeffs.transpose(0, 1, 3, 2), heads, tails,
     )
+    image = pl.pallas_call(
+        hand_out,
+        out_shape=jax.ShapeDtypeStruct((out_rows, width), BF16),
+        in_specs=[hbm],
+        out_specs=hbm,
+        scratch_shapes=[dma((COPIES,))],
+        compiler_params=pltpu.CompilerParams(vmem_limit_bytes=63 * 1024 * 1024),
+    )(image)
     return image.reshape(TILE_DEV, 2, AZ, width)
 
 

time: 32.9 us -> 93.5 us (2.84)
  Pallas kernels: 27.7 us -> 91.4 us
  local copies, waits for them, and re-layouts: 5.03 us -> 1.88 us
    pallas_call x0 -> x1, Pallas kernels: none -> 64.7 us  [body(): pl.pallas_call(hand_out, out_shape=jax.ShapeDtypeStruct((out_rows, width)...]
    unnamed x1 -> x0, local copies, waits for them, and re-layouts: 3.16 us -> none
    pallas_call x1, Pallas kernels: 27.7 us -> 26.7 us  [body(): pl.pallas_call(functools.partial(beam_kernel, n_pulse, n_range, blocks, s...]
where the time goes in v6:
time: 93.5 us; the launch traced here: 93.3 us
  Pallas kernels  91.4 us (98%)
  local copies, waits for them, and re-layouts  1.88 us (2%)
    pallas_call x1, Pallas kernels, body(): pl.pallas_call(hand_out, out_shape=jax.ShapeDtypeStruct((out_rows, width)...  64.7 us
    pallas_call x1, Pallas kernels, body(): pl.pallas_call(functools.partial(beam_kernel, n_pulse, n_range, blocks, s...  26.7 us
    slice x1, local copies, waits for them, and re-layouts, body(): tails = echoes[:, :, width - LANES:].reshape(2 * pulses, LANES)  1.88 us

profile of v6, /device:TPU:1, one launch (start us, length us, event | category | flops | bytes accessed | tf_op | source)
XLA Modules:
  0.0 93.3 jit_solution(16902938926514348763)
XLA Ops:
  0.0 1.9 %fusion = (bf16[256,2,128]{2,1,0:T(2,128)(2,1)}, bf16[256,2,128]{2,1,0:T(2,128)(2,1)}) fusion(bf16[256,2,2048]{2,1,0:T(2,128)(2,1)} %param.8), kind=kLoop, calls=%fused_computation | loop fusion | bytes 524288 | tf_op jit(solution)/shard_map/slice | solution.py:356
  1.9 26.7 %shard_map.82.image = bf16[512,2048]{1,0:T(8,128)(2,1)} custom-call(bf16[256,32,128]{2,1,0:T(8,128)(2,1)} %bitcast.14, s32[1,256]{1,0:T(1,128)} %bitcast.20, f32[8,256]{1,0:T(8,128)} %bitcast.18, f32[1,256]{1,0:T(1,128)} %bitcast.21, f32[1,256]{1,0:T(1,128)} %bitcast.22, bf16[16,32]{1,0:T(8,128)(2,1)} %bitcast.19, s32[16,32]{1,0:T(8,128)} %footprint_in.1, ...), custom_call_target="tpu_custom_call" | custom-call | tf_op jit(solution)/shard_map/pallas_call | solution.py:362
  28.6 64.7 %shard_map.83 = bf16[512,2048]{1,0:T(8,128)(2,1)} custom-call(bf16[512,2048]{1,0:T(8,128)(2,1)} %shard_map.82.image), custom_call_target="tpu_custom_call" | custom-call | tf_op jit(solution)/shard_map/pallas_call | solution.py:412

commit v7 on v6

--- a/solution.py
+++ b/solution.py
@@ -334,15 +334,19 @@
         to_right().wait_send()
 
 
-def hand_out(image, out, sems):
+def hand_out(image, out, held, in_sems, out_sems):
     rows = image.shape[0] // COPIES
-    copies = [
-        pltpu.make_async_copy(image.at[n * rows:(n + 1) * rows], out.at[n * rows:(n + 1) * rows], sems.at[n])
-        for n in range(COPIES)
-    ]
-    for copy in copies:
+    into, onward = [], []
+    for n in range(COPIES):
+        part = slice(n * rows, (n + 1) * rows)
+        into.append(pltpu.make_async_copy(image.at[part], held.at[part], in_sems.at[n]))
+        onward.append(pltpu.make_async_copy(held.at[part], out.at[part], out_sems.at[n]))
+    for copy in into:
         copy.start()
-    for copy in copies:
+    for first, second in zip(into, onward):
+        first.wait()
+        second.start()
+    for copy in onward:
         copy.wait()
 
 
@@ -414,7 +418,7 @@
         out_shape=jax.ShapeDtypeStruct((out_rows, width), BF16),
         in_specs=[hbm],
         out_specs=hbm,
-        scratch_shapes=[dma((COPIES,))],
+        scratch_shapes=[pltpu.VMEM((out_rows, width), BF16), dma((COPIES,)), dma((COPIES,))],
         compiler_params=pltpu.CompilerParams(vmem_limit_bytes=63 * 1024 * 1024),
     )(image)
     return image.reshape(TILE_DEV, 2, AZ, width)

time: 93.5 us -> 31.2 us (0.33)
  Pallas kernels: 91.4 us -> 29.1 us
    pallas_call x1, Pallas kernels: 64.7 us -> 2.39 us  [body(): pl.pallas_call(hand_out, out_shape=jax.ShapeDtypeStruct((out_rows, width)...]
where the time goes in v7:
time: 31.2 us; the launch traced here: 31 us
  Pallas kernels  29.1 us (93%)
  local copies, waits for them, and re-layouts  1.88 us (6%)
    pallas_call x1, Pallas kernels, body(): pl.pallas_call(functools.partial(beam_kernel, n_pulse, n_range, blocks, s...  26.7 us
    pallas_call x1, Pallas kernels, body(): pl.pallas_call(hand_out, out_shape=jax.ShapeDtypeStruct((out_rows, width)...  2.39 us
    slice x1, local copies, waits for them, and re-layouts, body(): tails = echoes[:, :, width - LANES:].reshape(2 * pulses, LANES)  1.88 us

profile of v7, /device:TPU:1, one launch (start us, length us, event | category | flops | bytes accessed | tf_op | source)
XLA Modules:
  0.0 31.0 jit_solution(10893841819564825289)
XLA Ops:
  0.0 1.9 %fusion = (bf16[256,2,128]{2,1,0:T(2,128)(2,1)}, bf16[256,2,128]{2,1,0:T(2,128)(2,1)}) fusion(bf16[256,2,2048]{2,1,0:T(2,128)(2,1)} %param.8), kind=kLoop, calls=%fused_computation | loop fusion | bytes 524288 | tf_op jit(solution)/shard_map/slice | solution.py:360
  1.9 26.7 %shard_map.82.image = bf16[512,2048]{1,0:T(8,128)(2,1)} custom-call(bf16[256,32,128]{2,1,0:T(8,128)(2,1)} %bitcast.14, s32[1,256]{1,0:T(1,128)} %bitcast.20, f32[8,256]{1,0:T(8,128)} %bitcast.18, f32[1,256]{1,0:T(1,128)} %bitcast.21, f32[1,256]{1,0:T(1,128)} %bitcast.22, bf16[16,32]{1,0:T(8,128)(2,1)} %bitcast.19, s32[16,32]{1,0:T(8,128)} %footprint_in.1, ...), custom_call_target="tpu_custom_call" | custom-call | tf_op jit(solution)/shard_map/pallas_call | solution.py:366
  28.6 2.4 %shard_map.83 = bf16[512,2048]{1,0:T(8,128)(2,1)} custom-call(bf16[512,2048]{1,0:T(8,128)(2,1)} %shard_map.82.image), custom_call_target="tpu_custom_call" | custom-call | tf_op jit(solution)/shard_map/pallas_call | solution.py:416

commit v8 on v7

--- a/solution.py
+++ b/solution.py
@@ -137,6 +137,27 @@
         d_im[span, :] = column(step_im)
         reach[span, :] = column(shift_values) + lane + float(LANES - TAPS // 2 + 1)
 
+    n_rows = n_pulse * subs * 2 * BEAMS
+    row = lax.broadcasted_iota(jnp.int32, (n_rows, FOOT), 0)
+    block_row = row // (2 * BEAMS)
+    beam = ((block_row % n_pulse) * subs + block_row // n_pulse) * BEAMS + row % BEAMS
+    is_im = (row // BEAMS) % 2
+    for load in loads[7:]:
+        load.wait()
+    for t in range(TILE_DEV):
+        ids = footprint[pl.ds(me * TILE_DEV + t, 1), :]
+        hit = beam == ids
+        hot_re = jnp.where(hit & (is_im == 0), 1.0, 0.0).astype(BF16)
+        hot_im = jnp.where(hit & (is_im == 1), 1.0, 0.0).astype(BF16)
+        c_re = jnp.transpose(coeffs[t, 0].astype(F32)).astype(BF16)
+        c_im = jnp.transpose(coeffs[t, 1].astype(F32)).astype(BF16)
+
+        def spread(a, b):
+            return lax.dot_general(a, b, (((1,), (1,)), ((), ())), preferred_element_type=F32)
+
+        dense[t * 2 * AZ:t * 2 * AZ + AZ, :] = (spread(c_re, hot_re) - spread(c_im, hot_im)).astype(BF16)
+        dense[t * 2 * AZ + AZ:(t + 1) * 2 * AZ, :] = (spread(c_im, hot_re) + spread(c_re, hot_im)).astype(BF16)
+
     @pl.when(has_left)
     def _():
         to_right().wait_recv()
@@ -249,27 +270,6 @@
         return carry
 
     lax.fori_loop(0, subs, one_sub, 0)
-    n_rows = n_pulse * subs * 2 * BEAMS
-    row = lax.broadcasted_iota(jnp.int32, (n_rows, FOOT), 0)
-    block_row = row // (2 * BEAMS)
-    beam = ((block_row % n_pulse) * subs + block_row // n_pulse) * BEAMS + row % BEAMS
-    is_im = (row // BEAMS) % 2
-    for load in loads[7:]:
-        load.wait()
-    for t in range(TILE_DEV):
-        ids = footprint[pl.ds(me * TILE_DEV + t, 1), :]
-        hit = beam == ids
-        hot_re = jnp.where(hit & (is_im == 0), 1.0, 0.0).astype(BF16)
-        hot_im = jnp.where(hit & (is_im == 1), 1.0, 0.0).astype(BF16)
-        c_re = jnp.transpose(coeffs[t, 0].astype(F32)).astype(BF16)
-        c_im = jnp.transpose(coeffs[t, 1].astype(F32)).astype(BF16)
-
-        def spread(a, b):
-            return lax.dot_general(a, b, (((1,), (1,)), ((), ())), preferred_element_type=F32)
-
-        dense[t * 2 * AZ:t * 2 * AZ + AZ, :] = (spread(c_re, hot_re) - spread(c_im, hot_im)).astype(BF16)
-        dense[t * 2 * AZ + AZ:(t + 1) * 2 * AZ, :] = (spread(c_im, hot_re) + spread(c_re, hot_im)).astype(BF16)
-
     def landed(first, last):
         def one(s, carry):
             sib_copy(s).wait_recv()

time: 31.2 us -> 31.2 us (level)
  no operation moved by 1% of the time
where the time goes in v8:
time: 31.2 us; the launch traced here: 31 us
  Pallas kernels  29.1 us (93%)
  local copies, waits for them, and re-layouts  1.88 us (6%)
    pallas_call x1, Pallas kernels, body(): pl.pallas_call(functools.partial(beam_kernel, n_pulse, n_range, blocks, s...  26.7 us
    pallas_call x1, Pallas kernels, body(): pl.pallas_call(hand_out, out_shape=jax.ShapeDtypeStruct((out_rows, width)...  2.39 us
    slice x1, local copies, waits for them, and re-layouts, body(): tails = echoes[:, :, width - LANES:].reshape(2 * pulses, LANES)  1.88 us

profile of v8, /device:TPU:1, one launch (start us, length us, event | category | flops | bytes accessed | tf_op | source)
XLA Modules:
  0.0 31.0 jit_solution(4472256627291303456)
XLA Ops:
  0.0 1.9 %fusion = (bf16[256,2,128]{2,1,0:T(2,128)(2,1)}, bf16[256,2,128]{2,1,0:T(2,128)(2,1)}) fusion(bf16[256,2,2048]{2,1,0:T(2,128)(2,1)} %param.8), kind=kLoop, calls=%fused_computation | loop fusion | bytes 524288 | tf_op jit(solution)/shard_map/slice | solution.py:360
  1.9 26.7 %shard_map.82.image = bf16[512,2048]{1,0:T(8,128)(2,1)} custom-call(bf16[256,32,128]{2,1,0:T(8,128)(2,1)} %bitcast.14, s32[1,256]{1,0:T(1,128)} %bitcast.20, f32[8,256]{1,0:T(8,128)} %bitcast.18, f32[1,256]{1,0:T(1,128)} %bitcast.21, f32[1,256]{1,0:T(1,128)} %bitcast.22, bf16[16,32]{1,0:T(8,128)(2,1)} %bitcast.19, s32[16,32]{1,0:T(8,128)} %footprint_in.1, ...), custom_call_target="tpu_custom_call" | custom-call | tf_op jit(solution)/shard_map/pallas_call | solution.py:366
  28.6 2.4 %shard_map.83 = bf16[512,2048]{1,0:T(8,128)(2,1)} custom-call(bf16[512,2048]{1,0:T(8,128)(2,1)} %shard_map.82.image), custom_call_target="tpu_custom_call" | custom-call | tf_op jit(solution)/shard_map/pallas_call | solution.py:416
